TPU v7x, 1024 devices: a whole 4x4x32 slice. The times are simulated.
1024 devices in a mesh: expert: 64 (over z, core), fsdp: 16 (over x, y).
Axes of the slice: x: 4, y: 4, z: 32, core: 2. Of those that a mesh axis runs over, the one named last changes fastest.
Arguments:
- tokens: bfloat16 [2048, 2048], P('expert', 'fsdp'), may hold values from -6 to 6
- target: bfloat16 [2048, 2048], P('expert', 'fsdp'), may hold values from -6 to 6
- expert_ids: int32 [2048, 8], P('expert'), may hold values from 0 to 63, all different within a row; in each aligned block of 32 rows (0 to 31, 32 to 63, ...) at most 7 rows name the same one
- route_weights: float32 [2048, 8], P('expert'), may hold values from 0.05 to 0.3
- w_gate: bfloat16 [64, 768, 2048], P('expert', 'fsdp'), may hold values from -0.1875 to 0.1875
- w_up: bfloat16 [64, 768, 2048], P('expert', 'fsdp'), may hold values from -0.1875 to 0.1875
- w_down: bfloat16 [64, 768, 2048], P('expert', 'fsdp'), may hold values from -0.3125 to 0.3125
Outputs:
- layer_out: bfloat16 [2048, 2048], P('expert', 'fsdp')
- grad_tokens: bfloat16 [2048, 2048], P('expert', 'fsdp')
- grad_route: float32 [2048, 8], P('expert')
- grad_gate: float32 [64, 768, 2048], P('expert', 'fsdp')
- grad_up: float32 [64, 768, 2048], P('expert', 'fsdp')
- grad_down: float32 [64, 768, 2048], P('expert', 'fsdp')
Inputs may be any that keep to these rules, and one draw needn't show every extreme that they name: `expert_ids`: each row names 8 different experts. In each aligned block of 32 rows (the rows of one index of the expert axis) no expert is named by more than 7 rows, a bound that some block reaches.
All inputs are finite; a program needn't handle non-finite values.
Results may differ from a plain program's by a relative error of at most 0.022.
Values may be sent and summed in bfloat16 or wider, within the bound.
No kernel may reach another device: no remote copies, remote signals or barrier semaphores. Data moves between devices by JAX's collectives and lax.ppermute only.
A program may use at most 64 MiB of HBM per device.

v0:
```python
import jax
import jax.numpy as jnp
from jax import lax
from jax.sharding import PartitionSpec as P


def route_tables(expert_ids, route_weights, experts_all, capacity):
    group_size, route_count = expert_ids.shape
    flat_ids = expert_ids.reshape(group_size * route_count)
    onehot = (flat_ids[:, None] == jnp.arange(experts_all, dtype=jnp.int32)[None, :]).astype(
        jnp.int32
    )
    before = jnp.cumsum(onehot, axis=0) - onehot
    route_rank = jnp.sum(before * onehot, axis=1)
    slot_index = flat_ids * capacity + route_rank
    route_slot = (
        slot_index[:, None] == jnp.arange(experts_all * capacity, dtype=jnp.int32)[None, :]
    ).astype(jnp.float32)
    route_token = jnp.arange(group_size * route_count, dtype=jnp.int32) // route_count
    token_table = (route_token[:, None] == jnp.arange(group_size, dtype=jnp.int32)[None, :]).astype(
        jnp.float32
    )
    placement = jnp.einsum("rs,rg->sg", route_slot, token_table, precision=lax.Precision.HIGHEST)
    weighted = jnp.einsum(
        "rs,rg->sg",
        route_slot * route_weights.reshape(-1)[:, None],
        token_table,
        precision=lax.Precision.HIGHEST,
    )
    return (placement, weighted, route_slot)


def send_rows(values, spread_table, n_expert, exp_count, capacity):
    features = lax.all_gather(values, "fsdp", axis=1, tiled=True)
    slot_rows = jnp.dot(
        spread_table, features.astype(jnp.float32), precision=lax.Precision.HIGHEST
    ).astype(jnp.bfloat16)
    slot_rows = slot_rows.reshape(n_expert, exp_count, capacity, features.shape[1])
    return lax.all_to_all(slot_rows, "expert", split_axis=0, concat_axis=0, tiled=True)


def collect(partial_out):
    reduced = lax.psum_scatter(partial_out, "fsdp", scatter_dimension=3, tiled=True).astype(
        jnp.float32
    )
    returned = lax.all_to_all(
        reduced.astype(jnp.bfloat16), "expert", split_axis=0, concat_axis=0, tiled=True
    ).astype(reduced.dtype)
    return returned.reshape(-1, returned.shape[3])


def shards(tokens, target, expert_ids, route_weights, w_gate, w_up, w_down):
    n_expert = lax.axis_size("expert")
    group_size, route_count = expert_ids.shape
    exp_count = w_gate.shape[0]
    experts_all = exp_count * n_expert
    mean_load = route_count * group_size // experts_all
    capacity = min(group_size, mean_load + mean_load // 2 + 1)
    placement, weighted, route_slot = route_tables(expert_ids, route_weights, experts_all, capacity)
    rows = send_rows(tokens, placement, n_expert, exp_count, capacity)
    gate_pre = jnp.einsum("neck,efk->necf", rows, w_gate, preferred_element_type=jnp.float32)
    up_pre = jnp.einsum("neck,efk->necf", rows, w_up, preferred_element_type=jnp.float32)
    sigmoid_gate = jax.nn.sigmoid(gate_pre)
    hidden = (gate_pre * sigmoid_gate * up_pre).astype(jnp.bfloat16)
    partial_out = jnp.einsum(
        "necf,efk->neck", hidden, w_down, preferred_element_type=jnp.float32
    ).astype(jnp.bfloat16)
    summed = collect(partial_out)
    layer_out = jnp.einsum("sg,sk->gk", weighted, summed, precision=lax.Precision.HIGHEST).astype(
        jnp.bfloat16
    )
    resid = (layer_out.astype(jnp.float32) - target.astype(jnp.float32)).astype(jnp.bfloat16)
    token_resid = jnp.dot(placement, resid.astype(jnp.float32), precision=lax.Precision.HIGHEST)
    slot_dot = jnp.sum(summed * token_resid, axis=1)
    route_part = jnp.dot(route_slot, slot_dot, precision=lax.Precision.HIGHEST).reshape(
        group_size, route_count
    )
    grad_route = lax.psum(route_part, "fsdp")
    scaled_rows = send_rows(resid, weighted, n_expert, exp_count, capacity)
    delta_hidden = jnp.einsum(
        "neck,efk->necf", scaled_rows, w_down, preferred_element_type=jnp.float32
    )
    delta_gate = (
        delta_hidden * up_pre * sigmoid_gate * (1.0 + gate_pre * (1.0 - sigmoid_gate))
    ).astype(jnp.bfloat16)
    delta_up = (delta_hidden * gate_pre * sigmoid_gate).astype(jnp.bfloat16)
    grad_gate = jnp.einsum("necf,neck->efk", delta_gate, rows, preferred_element_type=jnp.float32)
    grad_up = jnp.einsum("necf,neck->efk", delta_up, rows, preferred_element_type=jnp.float32)
    grad_down = jnp.einsum(
        "necf,neck->efk", hidden, scaled_rows, preferred_element_type=jnp.float32
    )
    back_part = jnp.einsum("necf,efk->neck", delta_gate, w_gate, preferred_element_type=jnp.float32)
    back_part = (
        back_part + jnp.einsum("necf,efk->neck", delta_up, w_up, preferred_element_type=jnp.float32)
    ).astype(jnp.bfloat16)
    back_summed = collect(back_part)
    grad_tokens = jnp.einsum(
        "sg,sk->gk", placement, back_summed, precision=lax.Precision.HIGHEST
    ).astype(jnp.bfloat16)
    return (layer_out, grad_tokens, grad_route, grad_gate, grad_up, grad_down)


def solution(mesh):
    return jax.shard_map(
        shards,
        mesh=mesh,
        in_specs=(
            P("expert", "fsdp"),
            P("expert", "fsdp"),
            P("expert", None),
            P("expert", None),
            P("expert", "fsdp", None),
            P("expert", "fsdp", None),
            P("expert", "fsdp", None),
        ),
        out_specs=(
            P("expert", "fsdp"),
            P("expert", "fsdp"),
            P("expert", None),
            P("expert", "fsdp", None),
            P("expert", "fsdp", None),
            P("expert", "fsdp", None),
        ),
        check_vma=False,
    )
```

profile of v0, /device:TPU:1, one launch (start us, length us, event | category | flops | bytes accessed | tf_op | source)
XLA Modules:
  0.0 848.7 jit_solution(12816745407971414303)
XLA Ops:
  7.2 0.0 copy-start
  7.2 0.0 reduce-scatter.7.cloned.1.call-start
  7.2 0.8 copy.25
  8.0 0.1 reshape.126
  8.1 0.1 eq.65
  8.2 0.6 reduce-window.6
  8.8 0.2 slice_reduce_fusion
  9.1 0.1 fusion.51
  9.2 19.4 %all_gather.6 = bf16[32,2048]{1,0:T(8,128)(2,1)S(1)} all-gather(bf16[32,128]{1,0:T(8,128)(2,1)} %param.7), channel_id=1, replica_groups=mesh['expert'=64,'fsdp'=16] {'fsdp'}, dimensions={1}, use_global_device_ids=true | all-gather | bytes 139264 | tf_op jit(solution)/shard_map/all_gather | solution.py:34
  28.6 0.3 fusion.29
  28.9 2.9 convolution_convert_fusion.2
  31.8 2.5 reshape.128
  34.3 0.0 copy-start.4
  34.3 232.6 %all_to_all.20 = bf16[64,1,7,2048]{3,2,1,0:T(8,128)(2,1)S(1)} all-to-all(bf16[64,1,7,2048]{3,2,1,0:T(8,128)(2,1)S(1)} %bitcast.142), channel_id=1, replica_groups=mesh['expert'=64,'fsdp'=16] {'expert'}, dimensions={0} | all-to-all | bytes 3670016 | tf_op jit(solution)/shard_map/all_to_all | solution.py:39
  266.9 0.0 copy-done.4
  266.9 2.2 fusion.13
  269.1 0.0 copy-done.5
  269.1 2.8 multiply_convert_fusion.2
  271.9 0.0 copy-done.1
  271.9 0.0 copy-done
  271.9 0.7 fusion
  272.6 4.3 copy.37
  276.9 6.3 reshape.149
  283.2 0.0 reduce-scatter.7.cloned.1.call-update
  283.2 90.3 %reduce-scatter.7.cloned.1.call-done = bf16[128,448]{1,0:T(8,128)(2,1)} async-done(((bf16[2048,448]{1,0:T(8,128)(2,1)}), bf16[128,448]{1,0:T(8,128)(2,1)}) %reduce-scatter.7.cloned.1.call-update) | async-done | bytes 114704
  373.5 1.1 reshape.150
  374.6 0.9 copy.31
  375.5 25.4 %all-to-all-start.1 = ((bf16[64,1,7,128]{3,2,1,0:T(8,128)(2,1)}), bf16[64,1,7,128]{3,2,1,0:T(8,128)(2,1)S(1)}, u32[]{:S(2)}, u32[]{:S(2)}) async-start(bf16[64,1,7,128]{3,2,1,0:T(8,128)(2,1)} %copy.31), calls=%async_computation.1 | async-start | bytes 262144 | tf_op jit(solution)/shard_map/all_to_all | solution.py:46
  401.0 0.0 reduce-scatter.9.cloned.1.call-start
  401.0 0.0 copy-done.7
  401.0 0.1 copy.28
  401.1 0.1 mul.58
  401.2 0.4 fusion.27
  401.6 30.0 %all-to-all-done.1 = bf16[64,1,7,128]{3,2,1,0:T(8,128)(2,1)S(1)} async-done(((bf16[64,1,7,128]{3,2,1,0:T(8,128)(2,1)}), bf16[64,1,7,128]{3,2,1,0:T(8,128)(2,1)S(1)}, u32[]{:S(2)}, u32[]{:S(2)}) %all-to-all-start.1) | async-done | bytes 114720 | tf_op jit(solution)/shard_map/all_to_all | solution.py:46
  431.7 0.0 copy-done.6
  431.7 0.8 subtract_convert_fusion
  432.5 17.8 %all_gather.7 = bf16[32,2048]{1,0:T(8,128)(2,1)S(1)} all-gather(bf16[32,128]{1,0:T(8,128)(2,1)S(1)} %get-tuple-element.10), channel_id=1, replica_groups=mesh['expert'=64,'fsdp'=16] {'fsdp'}, dimensions={1}, use_global_device_ids=true | all-gather | bytes 139264 | tf_op jit(solution)/shard_map/all_gather | solution.py:34
  450.3 2.9 convolution_convert_fusion
  453.2 2.5 reshape.135
  455.7 0.0 copy-start.8
  455.8 207.3 %all_to_all.21 = bf16[64,1,7,2048]{3,2,1,0:T(8,128)(2,1)S(1)} all-to-all(bf16[64,1,7,2048]{3,2,1,0:T(8,128)(2,1)S(1)} %bitcast.143), channel_id=1, replica_groups=mesh['expert'=64,'fsdp'=16] {'expert'}, dimensions={0} | all-to-all | bytes 3670016 | tf_op jit(solution)/shard_map/all_to_all | solution.py:39
  663.1 0.0 copy-done.8
  663.1 2.2 multiply_convert_fusion
  665.3 0.7 fusion.40
  665.9 0.0 copy-done.3
  665.9 0.7 fusion.1
  666.6 4.3 copy.39
  670.9 6.4 reshape.151
  677.2 0.0 reduce-scatter.9.cloned.1.call-update
  677.2 0.0 copy-start.2
  677.3 0.1 reduce_sum.21
  677.4 0.5 fusion.22
  677.8 90.0 %reduce-scatter.9.cloned.1.call-done = bf16[128,448]{1,0:T(8,128)(2,1)} async-done(((bf16[2048,448]{1,0:T(8,128)(2,1)}), bf16[128,448]{1,0:T(8,128)(2,1)}) %reduce-scatter.9.cloned.1.call-update) | async-done | bytes 114704
  767.8 1.1 reshape.152
  768.9 0.8 copy.34
  769.7 25.5 %all-to-all-start.3 = ((bf16[64,1,7,128]{3,2,1,0:T(8,128)(2,1)}), bf16[64,1,7,128]{3,2,1,0:T(8,128)(2,1)S(1)}, u32[]{:S(2)}, u32[]{:S(2)}) async-start(bf16[64,1,7,128]{3,2,1,0:T(8,128)(2,1)} %copy.34), calls=%async_computation.3 | async-start | bytes 262144 | tf_op jit(solution)/shard_map/all_to_all | solution.py:46
  795.2 1.9 fusion.30
  797.1 0.1 copy.36
  797.2 33.8 %psum.7 = f32[32,8]{0,1:T(8,128)} all-reduce(f32[32,8]{0,1:T(8,128)S(1)} %bitcast.146), channel_id=1, replica_groups=mesh['expert'=64,'fsdp'=16] {'fsdp'}, use_global_device_ids=true, to_apply=%region_6.7 | all-reduce | flops 256 | bytes 2048 | tf_op jit(solution)/shard_map/psum | solution.py:78
  830.9 4.4 convolution_bitcast_fusion
  835.4 2.8 convolution_bitcast_fusion.1
  838.2 2.8 convolution_bitcast_fusion.2
  841.0 0.0 all-to-all-done.3
  841.1 0.8 convolution_convert_fusion.3
  (13 shorter events, 0.2 us)
Async XLA Ops:
  7.2 264.8 %copy-start = (bf16[1,48,2048]{2,1,0:T(8,128)(2,1)S(1)}, bf16[1,48,2048]{2,1,0:T(8,128)(2,1)}, u32[]{:S(2)}) copy-start(bf16[1,48,2048]{2,1,0:T(8,128)(2,1)} %param.13) | copy-start | bytes 589828
  7.2 366.4 %reduce-scatter.7.cloned.1.call-start = ((), (), s32[]{:S(2)}) async-start(), calls=%async_computation.6 | async-start | bytes 2228224
  34.3 232.6 %copy-start.4 = (bf16[1,48,2048]{2,1,0:T(8,128)(2,1)S(1)}, bf16[1,48,2048]{2,1,0:T(8,128)(2,1)}, u32[]{:S(2)}) copy-start(bf16[1,48,2048]{2,1,0:T(8,128)(2,1)} %param.11) | copy-start | bytes 589828
  266.9 5.0 copy-start.1
  266.9 2.2 copy-start.5
  283.2 117.8 %copy-start.7 = (f32[32,8]{0,1:T(8,128)S(1)}, f32[32,8]{0,1:T(8,128)}, u32[]{:S(2)}) copy-start(f32[32,8]{0,1:T(8,128)} %param.10) | copy-start | bytes 3076
  283.2 148.5 %copy-start.6 = (bf16[32,128]{1,0:T(8,128)(2,1)S(1)}, bf16[32,128]{1,0:T(8,128)(2,1)}, u32[]{:S(2)}) copy-start(bf16[32,128]{1,0:T(8,128)(2,1)} %param.8) | copy-start | bytes 24580
  375.5 56.1 %all-to-all-start.1 = ((bf16[64,1,7,128]{3,2,1,0:T(8,128)(2,1)}), bf16[64,1,7,128]{3,2,1,0:T(8,128)(2,1)S(1)}, u32[]{:S(2)}, u32[]{:S(2)}) async-start(bf16[64,1,7,128]{3,2,1,0:T(8,128)(2,1)} %copy.31), calls=%async_computation.1 | async-start | bytes 262144 | tf_op jit(solution)/shard_map/all_to_all | solution.py:46
  401.0 366.8 %reduce-scatter.9.cloned.1.call-start = ((), (), s32[]{:S(2)}) async-start(), calls=%async_computation.7 | async-start | bytes 2228224
  455.7 207.3 %copy-start.8 = (f32[64,1,7,48]{0,3,2,1:T(8,128)S(1)}, f32[64,1,7,48]{0,3,2,1:T(8,128)}, u32[]{:S(2)}) copy-start(f32[64,1,7,48]{0,3,2,1:T(8,128)} %get-tuple-element.9) | copy-start | bytes 258052
  663.1 2.9 copy-start.3
  677.2 158.1 %copy-start.2 = (bf16[64,1,7,2048]{3,2,1,0:T(8,128)(2,1)S(1)}, bf16[64,1,7,2048]{3,2,1,0:T(8,128)(2,1)}, u32[]{:S(2)}) copy-start(bf16[64,1,7,2048]{3,2,1,0:T(8,128)(2,1)} %copy-done.1) | copy-start | bytes 5505028
  769.7 71.3 %all-to-all-start.3 = ((bf16[64,1,7,128]{3,2,1,0:T(8,128)(2,1)}), bf16[64,1,7,128]{3,2,1,0:T(8,128)(2,1)S(1)}, u32[]{:S(2)}, u32[]{:S(2)}) async-start(bf16[64,1,7,128]{3,2,1,0:T(8,128)(2,1)} %copy.34), calls=%async_computation.3 | async-start | bytes 262144 | tf_op jit(solution)/shard_map/all_to_all | solution.py:46
Sparse Core Ops, SparseCore 0:
  283.4 90.1 reduce-scatter.6
  677.4 90.3 reduce-scatter.8
where the time goes:
time: 853 us; the launch traced here: 849 us
  blocking collectives  511 us (60%)
  waiting for transfers between devices  210 us (25%)
  starting transfers between devices  51 us (6%)
  local copies, waits for them, and re-layouts  31.8 us (4%)
  matrix products  29.7 us (3%)
  between operations  14.2 us (2%)
    all_to_all x2, blocking collectives, send_rows(): lax.all_to_all(slot_rows, 'expert', split_axis=0, concat_axis=0, tiled=True)  440 us
    unnamed x4, waiting for transfers between devices  180 us
    all_to_all x2, starting transfers between devices, collect(): lax.all_to_all(reduced.astype(jnp.bfloat16), 'expert', split_axis=0, conc...  50.9 us
    all_gather x2, blocking collectives, send_rows(): features = lax.all_gather(values, 'fsdp', axis=1, tiled=True)  37.2 us
    psum x1, blocking collectives, shards(): grad_route = lax.psum(route_part, 'fsdp')  33.8 us
    all_to_all x2, waiting for transfers between devices, collect(): lax.all_to_all(reduced.astype(jnp.bfloat16), 'expert', split_axis=0, conc...  30 us
    unnamed x26, local copies, waits for them, and re-layouts  24.4 us
  transfers between devices with their start and end apart: 4, of which 3 were waited for; matrix products, arithmetic and copies ran while one was open for 2% of the time, Pallas kernels for 0%

commit v1 on v0

v1 whole, which is shorter than its diff:
```python
import functools

import jax
import jax.numpy as jnp
from jax import lax
from jax.experimental import pallas as pl
from jax.experimental.pallas import tpu as pltpu
from jax.sharding import Mesh, PartitionSpec as P

BF = jnp.bfloat16
F4 = jnp.float32
LANES = 128
HI = 8
CAP = 7


def dot(a, b, ca=1, cb=0):
    return lax.dot_general(a, b, (((ca,), (cb,)), ((), ())), preferred_element_type=F4)


def call(body, outs, *args, smem=(), flops=1e8, name=None):
    specs = [
        pl.BlockSpec(memory_space=pltpu.SMEM if i in smem else pltpu.VMEM)
        for i in range(len(args))
    ]
    nbytes = sum(a.size * a.dtype.itemsize for a in args)
    shapes = [jax.ShapeDtypeStruct(s, d) for s, d in outs]
    return pl.pallas_call(
        body,
        out_shape=shapes,
        in_specs=specs,
        out_specs=[pl.BlockSpec(memory_space=pltpu.VMEM) for _ in shapes],
        compiler_params=pltpu.CompilerParams(vmem_limit_bytes=40 * 1024 * 1024),
        cost_estimate=pl.CostEstimate(
            flops=int(flops), bytes_accessed=int(nbytes), transcendentals=0
        ),
        name=name,
    )(*args)


def lane(shape):
    return lax.broadcasted_iota(jnp.int32, shape, 1)


def roll(x, by):
    by = by % LANES
    return x if by == 0 else pltpu.roll(x, by, 1)


def split3(x, step):
    hi = x.astype(BF).astype(F4)
    rest = x - hi
    mid = rest.astype(BF).astype(F4)
    return hi + roll(mid, step) + roll(rest - mid, 2 * step)


def join3(x, step):
    return x + roll(x, -step) + roll(x, -2 * step)


def column_tile(column, h):
    at = lane((h, LANES))
    tile = jnp.zeros((h, LANES), F4)
    for c in range(CAP):
        tile = jnp.where(at == c, column[c * h : (c + 1) * h], tile)
    return tile


def scale_rows(rows, tile, h):
    return jnp.concatenate(
        [rows[c * h : (c + 1) * h] * tile[:, c : c + 1] for c in range(CAP)], axis=0
    )


def blocks_to_rows(x):
    return jnp.concatenate(
        [x[:, i * LANES : (i + 1) * LANES] for i in range(x.shape[1] // LANES)], axis=0
    )


def rows_to_blocks(x, rows):
    return jnp.concatenate(
        [x[i * rows : (i + 1) * rows] for i in range(x.shape[0] // rows)], axis=1
    )


def dispatch_body(base_ref, r_ref, m_ref, p_ref, ids_ref):
    h, l = r_ref.shape[0], m_ref.shape[0]
    g = 32
    width = h * g
    per = LANES // g
    at = lane((8, LANES))
    metas = [r_ref[i].astype(F4)[g : g + 8] for i in range(h)]

    def gathered(parts, start):
        out = []
        for q in range(h // per):
            acc = jnp.zeros((8, LANES), F4)
            for i in range(per):
                moved = roll(parts[q * per + i], i * g - start)
                acc = jnp.where(at // g == i, moved, acc)
            out.append(acc)
        return jnp.concatenate(out, axis=1)

    ids = gathered(metas, 0)
    weights = gathered([join3(m, g) for m in metas], g)
    ids_ref[...] = ids
    mine = (lax.broadcasted_iota(jnp.int32, (l, width), 0) + base_ref[0]).astype(F4)
    named = jnp.zeros((l, width), F4)
    weight_at = jnp.zeros((l, width), F4)
    for k in range(8):
        hit = ids[k : k + 1] == mine
        named = named + jnp.where(hit, 1.0, 0.0)
        weight_at = weight_at + jnp.where(hit, weights[k : k + 1], 0.0)
    row = lax.broadcasted_iota(jnp.int32, (width, width), 0)
    col = lane((width, width))
    before = jnp.where((row // g == col // g) & (row < col), 1.0, 0.0).astype(BF)
    rank = dot(named.astype(BF), before)
    rank = jnp.where(named > 0.0, rank, -1.0)
    block = lane((h, width)) // g == lax.broadcasted_iota(jnp.int32, (h, width), 0)
    x = jnp.concatenate([r_ref[i][:g] for i in range(h)], axis=0)
    for e in range(l):
        own = jnp.broadcast_to(rank[e : e + 1], (h, width))
        place = jnp.concatenate(
            [jnp.where(block & (own == float(c)), 1.0, 0.0) for c in range(8)], axis=0
        )
        column = jnp.sum(place * weight_at[e : e + 1], axis=1, keepdims=True)
        place = place.astype(BF)
        p_ref[e] = place
        rows = dot(place, x)
        tile = split3(column_tile(column, h), 8)
        m_ref[e] = jnp.concatenate([rows[: CAP * h], tile], axis=0).astype(BF)


def expert_in_body(r_ref, wg_ref, wu_ref, wd_ref, f_ref, w_ref):
    l, h = r_ref.shape[0], r_ref.shape[1] // 8
    fs = wg_ref.shape[0]
    rows = []
    for e in range(l):
        v = r_ref[e].astype(F4)
        rows.append(v[: CAP * h])
        w_ref[e] = join3(v[CAP * h :], 8)
    x = jnp.concatenate(rows, axis=0).astype(BF)
    for d in range(f_ref.shape[0]):
        part = pl.ds(d * LANES, LANES)
        f_ref[d, 0:fs] = wg_ref[:, part]
        f_ref[d, fs : 2 * fs] = wu_ref[:, part]
        f_ref[d, 2 * fs : 3 * fs] = wd_ref[:, part]
        f_ref[d, 3 * fs :] = x


def hidden_body(r_ref, wg_ref, wu_ref, gate_ref, up_ref, f_ref):
    n, fs = r_ref.shape[0], wg_ref.shape[0]
    slots = gate_ref.shape[1]
    held = r_ref.shape[1] - 3 * fs
    pad = jnp.zeros((slots - held, 2 * LANES), BF)
    total = jnp.zeros((2 * fs, slots), F4)
    for i in range(n // 2):
        x = jnp.concatenate([r_ref[2 * i, 3 * fs :], r_ref[2 * i + 1, 3 * fs :]], axis=1)
        x = jnp.concatenate([x, pad], axis=0)
        part = pl.ds(2 * i * LANES, 2 * LANES)
        w = jnp.concatenate([wg_ref[:, part], wu_ref[:, part]], axis=0)
        total = total + dot(w, x, 1, 1)
    gate, up = total[:fs], total[fs:]
    gate_ref[...] = gate
    up_ref[...] = up
    hidden = (gate * jax.nn.sigmoid(gate) * up).astype(BF)
    message = blocks_to_rows(hidden)
    for d in range(n):
        f_ref[d] = message


def expert_out_body(r_ref, wd_ref, w_ref, out_ref, h_ref, m_ref):
    n, fs = r_ref.shape[0], r_ref.shape[1] // 4
    l, h = w_ref.shape[0], w_ref.shape[1]
    hidden = jnp.concatenate([rows_to_blocks(r_ref[i], fs) for i in range(n)], axis=0)
    h_ref[...] = hidden
    out = dot(hidden, wd_ref[...], 0, 0)
    out_ref[...] = out
    for e in range(l):
        rows = out[e * CAP * h : (e + 1) * CAP * h]
        rows = scale_rows(rows, w_ref[e], h)
        m_ref[e] = jnp.concatenate([rows, jnp.zeros((h, LANES), F4)], axis=0).astype(BF)


def combine_body(r_ref, p_ref, m_ref):
    l, rows = r_ref.shape[0], r_ref.shape[1]
    x = jnp.concatenate([r_ref[i] for i in range(l)], axis=0)
    p = jnp.concatenate([p_ref[i] for i in range(l)], axis=0)
    y = dot(p, x, 0, 0).astype(BF)
    g = m_ref.shape[1]
    for i in range(m_ref.shape[0]):
        m_ref[i] = y[i * g : (i + 1) * g]


def resid_body(r_ref, t_ref, o_ref, m_ref):
    total = r_ref[0].astype(F4)
    for i in range(1, r_ref.shape[0]):
        total = total + r_ref[i].astype(F4)
    layer = total.astype(BF)
    o_ref[...] = layer
    resid = (layer.astype(F4) - t_ref[...].astype(F4)).astype(BF)
    for i in range(m_ref.shape[0]):
        m_ref[i] = resid


def redispatch_body(r_ref, p_ref, m_ref):
    x = jnp.concatenate([r_ref[i] for i in range(r_ref.shape[0])], axis=0)
    for e in range(p_ref.shape[0]):
        m_ref[e] = dot(p_ref[e], x).astype(BF)


def delta_in_body(r_ref, w_ref, out_ref, wd_ref, f_ref, s_ref):
    l, h = w_ref.shape[0], w_ref.shape[1]
    n, fs = f_ref.shape[0], f_ref.shape[1] // 4
    slots = s_ref.shape[0]
    rows, tiles = [], []
    for e in range(l):
        resid = r_ref[e].astype(F4)[: CAP * h]
        out = out_ref[e * CAP * h : (e + 1) * CAP * h]
        column = jnp.sum(resid * out, axis=1, keepdims=True)
        tiles.append(split3(column_tile(column, h), 8))
        rows.append(scale_rows(resid, w_ref[e], h))
    rows.append(jnp.zeros((slots - l * CAP * h, LANES), F4))
    scaled = jnp.concatenate(rows, axis=0).astype(BF)
    s_ref[...] = scaled
    half = l // 2
    packed = roll(jnp.concatenate(tiles[:half], axis=0), 64) + roll(
        jnp.concatenate(tiles[half:], axis=0), 88
    )
    packed = jnp.concatenate([packed, jnp.zeros((fs - packed.shape[0], LANES), F4)], axis=0)
    for d in range(n):
        part = dot(wd_ref[d * fs : (d + 1) * fs], scaled, 1, 1)
        message = blocks_to_rows(part)
        last = message[3 * fs :] + packed
        f_ref[d] = jnp.concatenate([message[: 3 * fs], last], axis=0).astype(BF)


def grad_down_body(h_ref, s_ref, g_ref):
    n, fs = g_ref.shape[0], g_ref.shape[1] // 2
    for d in range(n):
        grad = dot(h_ref[d * fs : (d + 1) * fs], s_ref[...])
        hi = grad.astype(BF)
        g_ref[d, :fs] = hi
        g_ref[d, fs:] = (grad - hi.astype(F4)).astype(BF)


def delta_body(r_ref, gate_ref, up_ref, gd_ref, f_ref, dgu_ref, dot_ref):
    n, fs = f_ref.shape[0], gate_ref.shape[0]
    l, h = dot_ref.shape[0], dot_ref.shape[1]
    total = r_ref[0].astype(F4)
    for i in range(1, n):
        total = total + r_ref[i].astype(F4)
    packed = total[3 * fs : 3 * fs + l * h // 2]
    first, second = join3(roll(packed, -64), 8), join3(roll(packed, -88), 8)
    at = lane((h, LANES))
    for e in range(l):
        source = first if e < l // 2 else second
        i = e % (l // 2)
        dot_ref[e] = jnp.where(at < CAP, source[i * h : (i + 1) * h], 0.0)
    dh = rows_to_blocks(total, fs)
    gate, up = gate_ref[...], up_ref[...]
    s = jax.nn.sigmoid(gate)
    dgate = (dh * up * s * (1.0 + gate * (1.0 - s))).astype(BF)
    dup = (dh * gate * s).astype(BF)
    dgu = jnp.concatenate([dgate, dup], axis=0)
    dgu_ref[...] = dgu
    message = blocks_to_rows(dgu)
    for d in range(n):
        f_ref[d, : 8 * fs] = message
        f_ref[d, 8 * fs :] = gd_ref[d]


def back_body(r_ref, wgu_ref, dot_ref, m_ref):
    n, fs = r_ref.shape[0], r_ref.shape[1] // 10
    l, h = dot_ref.shape[0], dot_ref.shape[1]
    dgu = jnp.concatenate(
        [rows_to_blocks(r_ref[i, : 8 * fs], 2 * fs) for i in range(n)], axis=0
    )
    back = dot(dgu, wgu_ref[...], 0, 0)
    for e in range(l):
        rows = back[e * CAP * h : (e + 1) * CAP * h]
        m_ref[e] = jnp.concatenate([rows, split3(dot_ref[e], 8)], axis=0).astype(BF)


def grad_gate_body(r_ref, dgu_ref, gg_ref, gu_ref):
    n, fs = r_ref.shape[0], gg_ref.shape[0]
    dgu = dgu_ref[...]
    slots = dgu.shape[1]
    pad = jnp.zeros((slots - r_ref.shape[1] + 3 * fs, 2 * LANES), BF)
    for i in range(n // 2):
        x = jnp.concatenate([r_ref[2 * i, 3 * fs :], r_ref[2 * i + 1, 3 * fs :]], axis=1)
        grad = dot(dgu, jnp.concatenate([x, pad], axis=0))
        part = pl.ds(2 * i * LANES, 2 * LANES)
        gg_ref[:, part] = grad[:fs]
        gu_ref[:, part] = grad[fs:]


def grad_down_out_body(r_ref, gd_ref):
    fs = gd_ref.shape[0]
    for i in range(r_ref.shape[0]):
        hi, mid = r_ref[i, 8 * fs : 9 * fs], r_ref[i, 9 * fs :]
        gd_ref[:, i * LANES : (i + 1) * LANES] = hi.astype(F4) + mid.astype(F4)


def combine_back_body(base_ref, r_ref, p_ref, ids_ref, m_ref):
    l, hosts = r_ref.shape[0], m_ref.shape[0]
    h = hosts
    g = 32
    per = LANES // g
    x = jnp.concatenate([r_ref[i] for i in range(l)], axis=0)
    p = jnp.concatenate([p_ref[i] for i in range(l)], axis=0)
    y = dot(p, x, 0, 0)
    ids = ids_ref[...]
    routes = jnp.zeros(ids.shape, F4)
    for e in range(l):
        tile = join3(r_ref[e].astype(F4)[CAP * h :], 8)
        place = p_ref[e].astype(F4)
        acc = jnp.zeros((h, ids.shape[1]), F4)
        for c in range(CAP):
            acc = acc + place[c * h : (c + 1) * h] * tile[:, c : c + 1]
        at_token = jnp.sum(acc, axis=0, keepdims=True)
        mine = (base_ref[0] + e).astype(F4)
        routes = routes + jnp.where(ids == mine, at_token, 0.0)
    at = lane((8, LANES))
    for i in range(hosts):
        q = i // per
        own = roll(routes[:, q * LANES : (q + 1) * LANES], -(i % per) * g)
        own = split3(jnp.where(at < g, own, 0.0), g)
        m_ref[i] = jnp.concatenate(
            [y[i * g : (i + 1) * g], own, jnp.zeros((8, LANES), F4)], axis=0
        ).astype(BF)


def finish_body(r_ref, t_ref, g_ref):
    total = r_ref[0].astype(F4)
    for i in range(1, r_ref.shape[0]):
        total = total + r_ref[i].astype(F4)
    rows = t_ref.shape[0]
    t_ref[...] = total[:rows].astype(BF)
    g_ref[...] = join3(total[rows : rows + 8], rows)


def exchange(x, axis):
    return lax.all_to_all(x, axis, split_axis=0, concat_axis=0, tiled=True)


def shards(tokens, target, expert_ids, route_weights, w_gate, w_up, w_down):
    h, l, n = lax.axis_size("eh"), lax.axis_size("el"), lax.axis_size("fsdp")
    g, k = expert_ids.shape
    fs, d = w_gate.shape[1], w_gate.shape[2]
    df = tokens.shape[1]
    mean_load = k * g // (h * l)
    assert df == LANES and g == 32 and k == 8 and h % 8 == 0
    assert min(g, mean_load + mean_load // 2 + 1) == CAP
    wg, wu, wd = w_gate[0], w_up[0], w_down[0]
    held, slots = CAP * h * l, 8 * h * l
    base = (lax.axis_index("eh") * l).astype(jnp.int32).reshape(1)

    weights = route_weights.T
    hi = lax.reduce_precision(weights, 8, 7)
    mid = lax.reduce_precision(weights - hi, 8, 7)
    low = weights - hi - mid
    meta = jnp.concatenate([expert_ids.T.astype(F4), hi, mid, low], axis=1).astype(BF)
    first = jnp.concatenate([tokens, meta, jnp.zeros((8, LANES), BF)], axis=0)
    first = jnp.broadcast_to(first[None], (h,) + first.shape)
    got = exchange(first, "eh")
    message, place, ids = call(
        dispatch_body,
        [((l, 8 * h, df), BF), ((l, 8 * h, h * g), BF), ((8, h * g), F4)],
        base, got, smem=(0,), name="dispatch",
    )
    got = exchange(message, "el")
    message, w_tile = call(
        expert_in_body,
        [((n, 3 * fs + held, df), BF), ((l, h, LANES), F4)],
        got, wg, wu, wd, name="expert_in",
    )
    rows = exchange(message, "fsdp")
    gate, up, message = call(
        hidden_body,
        [((fs, slots), F4), ((fs, slots), F4), ((n, fs * slots // LANES, LANES), BF)],
        rows, wg, wu, name="hidden",
    )
    wgu_f = rows[:, : 2 * fs].reshape(n * 2 * fs, df)
    wd_f = rows[:, 2 * fs : 3 * fs].reshape(n * fs, df)
    got = exchange(message, "fsdp")
    out, hidden, message = call(
        expert_out_body,
        [((slots, df), F4), ((n * fs, slots), BF), ((l, 8 * h, df), BF)],
        got, wd_f, w_tile, name="expert_out",
    )
    got = exchange(message, "el")
    (message,) = call(combine_body, [((h, g, df), BF)], got, place, name="combine")
    got = exchange(message, "eh")
    layer_out, message = call(
        resid_body, [((g, df), BF), ((h, g, df), BF)], got, target, name="resid"
    )
    got = exchange(message, "eh")
    (message,) = call(
        redispatch_body, [((l, 8 * h, df), BF)], got, place, name="redispatch"
    )
    got = exchange(message, "el")
    message, scaled = call(
        delta_in_body,
        [((n, fs * slots // LANES, LANES), BF), ((slots, df), BF)],
        got, w_tile, out, wd_f, name="delta_in",
    )
    got = exchange(message, "fsdp")
    (grad_down_parts,) = call(
        grad_down_body, [((n, 2 * fs, df), BF)], hidden, scaled, name="grad_down"
    )
    message, dgu, dots = call(
        delta_body,
        [((n, 10 * fs, LANES), BF), ((2 * fs, slots), BF), ((l, h, LANES), F4)],
        got, gate, up, grad_down_parts, name="delta",
    )
    deltas = exchange(message, "fsdp")
    grad_gate, grad_up = call(
        grad_gate_body, [((fs, d), F4), ((fs, d), F4)], rows, dgu, name="grad_gate"
    )
    (message,) = call(
        back_body, [((l, 8 * h, df), BF)], deltas, wgu_f, dots, name="back"
    )
    got = exchange(message, "el")
    (grad_down,) = call(grad_down_out_body, [((fs, d), F4)], deltas, name="grad_down_out")
    (message,) = call(
        combine_back_body, [((h, g + 16, df), BF)],
        base, got, place, ids, smem=(0,), name="combine_back",
    )
    got = exchange(message, "eh")
    grad_tokens, grad_route = call(
        finish_body, [((g, df), BF), ((8, LANES), F4)], got, name="finish"
    )
    grad_route = grad_route[:, :g].T
    return (layer_out, grad_tokens, grad_route, grad_gate[None], grad_up[None], grad_down[None])


def solution(mesh):
    experts, fsdp = mesh.devices.shape
    split = Mesh(mesh.devices.reshape(HI, experts // HI, fsdp), ("eh", "el", "fsdp"))
    e = ("eh", "el")
    return jax.shard_map(
        shards,
        mesh=split,
        in_specs=(
            P(e, "fsdp"),
            P(e, "fsdp"),
            P(e, None),
            P(e, None),
            P(e, "fsdp", None),
            P(e, "fsdp", None),
            P(e, "fsdp", None),
        ),
        out_specs=(
            P(e, "fsdp"),
            P(e, "fsdp"),
            P(e, None),
            P(e, "fsdp", None),
            P(e, "fsdp", None),
            P(e, "fsdp", None),
        ),
        check_vma=False,
    )
```

time: 853 us -> 309 us (0.36)
  blocking collectives: 511 us -> 141 us
  waiting for transfers between devices: 210 us -> 86 us
  matrix products: 29.7 us -> 0 us
  local copies, waits for them, and re-layouts: 31.8 us -> 17.8 us
  between operations: 14.2 us -> 0.83 us
  Pallas kernels: 0 us -> 12.3 us
    all_to_all x2 -> x7, blocking collectives: 440 us -> 141 us  [exchange(): return lax.all_to_all(x, axis, split_axis=0, concat_axis=0, tiled=True)]
    unnamed x4 -> x0, waiting for transfers between devices: 180 us -> none
    all_to_all x2 -> x5, waiting for transfers between devices: 30 us -> 86 us  [exchange(): return lax.all_to_all(x, axis, split_axis=0, concat_axis=0, tiled=True)]
    all_gather x2 -> x0, blocking collectives: 37.2 us -> none  [send_rows(): features = lax.all_gather(values, 'fsdp', axis=1, tiled=True)]
    psum x1 -> x0, blocking collectives: 33.8 us -> none  [shards(): grad_route = lax.psum(route_part, 'fsdp')]
    dot_general x17 -> x0, matrix products: 29.7 us -> none  [the longest x2 5.78 us: send_rows(): jnp.dot(spread_table, features.astype(jnp.float32), precision=lax.Precisi...]
    pallas_call x0 -> x15, Pallas kernels: none -> 12.3 us  [call(): pl.pallas_call(body, out_shape=shapes, in_specs=specs, out_specs=[pl.Bloc...]
    unnamed x26 -> x40, local copies, waits for them, and re-layouts: 24.4 us -> 15.7 us
  transfers between devices with their start and end apart: 4 -> 5, of which waited for: 3 -> 5; matrix products, arithmetic and copies ran while one was open for 2% -> 0% of each run, Pallas kernels for 0% -> 1%
where the time goes in v1:
time: 309 us; the launch traced here: 304 us
  blocking collectives  141 us (46%)
  waiting for transfers between devices  86 us (28%)
  starting transfers between devices  44 us (14%)
  local copies, waits for them, and re-layouts  17.8 us (6%)
  Pallas kernels  12.3 us (4%)
    all_to_all x7, blocking collectives, exchange(): return lax.all_to_all(x, axis, split_axis=0, concat_axis=0, tiled=True)  141 us
    all_to_all x5, waiting for transfers between devices, exchange(): return lax.all_to_all(x, axis, split_axis=0, concat_axis=0, tiled=True)  86 us
    all_to_all x5, starting transfers between devices, exchange(): return lax.all_to_all(x, axis, split_axis=0, concat_axis=0, tiled=True)  44 us
    unnamed x40, local copies, waits for them, and re-layouts  15.7 us
    pallas_call x15, Pallas kernels, call(): pl.pallas_call(body, out_shape=shapes, in_specs=specs, out_specs=[pl.Bloc...  12.3 us
  transfers between devices with their start and end apart: 5, of which 5 were waited for; matrix products, arithmetic and copies ran while one was open for 0% of the time, Pallas kernels for 1%

profile of v1, /device:TPU:1, one launch (start us, length us, event | category | flops | bytes accessed | tf_op | source)
XLA Modules:
  0.0 303.9 jit_solution(8201972519044408148)
XLA Ops:
  0.6 0.7 fusion.1
  1.3 0.7 reduce-precision_convert_fusion.1
  2.0 0.1 pad.5.clone
  2.1 0.8 maximum_maximum_fusion
  2.9 0.7 broadcast_in_dim.19
  3.5 28.9 %all-to-all-start = ((bf16[8,48,128]{2,1,0:T(8,128)(2,1)}), bf16[8,48,128]{2,1,0:T(8,128)(2,1)S(1)}, u32[]{:S(2)}, u32[]{:S(2)}) async-start(bf16[8,48,128]{2,1,0:T(8,128)(2,1)} %broadcast_in_dim.19), calls=%async_computation | async-start | bytes 196608 | tf_op jit(solution)/shard_map/all_to_all | solution.py:345
  32.4 22.6 %all-to-all-done.r_ref = bf16[8,48,128]{2,1,0:T(8,128)(2,1)S(1)} async-done(((bf16[8,48,128]{2,1,0:T(8,128)(2,1)}), bf16[8,48,128]{2,1,0:T(8,128)(2,1)S(1)}, u32[]{:S(2)}, u32[]{:S(2)}) %all-to-all-start) | async-done | bytes 98336 | tf_op jit(solution)/shard_map/all_to_all | solution.py:345
  55.0 0.5 dispatch.1
  55.5 15.2 %all_to_all.60.r_ref = bf16[8,64,128]{2,1,0:T(8,128)(2,1)S(1)} all-to-all(bf16[8,64,128]{2,1,0:T(8,128)(2,1)S(1)} %get-tuple-element.28), channel_id=1, replica_groups=mesh['eh'=8,'el'=8,'fsdp'=16] {'el'}, dimensions={0} | all-to-all | bytes 262144 | tf_op jit(solution)/shard_map/all_to_all | solution.py:345
  70.7 0.9 copy-done.8
  71.6 0.9 copy-done.9
  72.5 0.9 copy-done.10
  73.4 0.3 expert_in.1
  73.8 37.0 %all_to_all.61.r_ref = bf16[16,592,128]{2,1,0:T(8,128)(2,1)S(1)} all-to-all(bf16[16,592,128]{2,1,0:T(8,128)(2,1)S(1)} %get-tuple-element.29), channel_id=1, replica_groups=mesh['eh'=8,'el'=8,'fsdp'=16] {'fsdp'}, dimensions={0} | all-to-all | bytes 4849664 | tf_op jit(solution)/shard_map/all_to_all | solution.py:345
  110.7 0.7 hidden.1
  111.5 0.0 copy-start.7
  111.5 0.9 copy-done.7
  112.4 0.6 copy-done.15
  113.0 0.6 copy-done.17
  113.7 3.7 %all-to-all-start.3 = ((bf16[16,192,128]{2,1,0:T(8,128)(2,1)}), bf16[16,192,128]{2,1,0:T(8,128)(2,1)S(1)}, u32[]{:S(2)}, u32[]{:S(2)}) async-start(bf16[16,192,128]{2,1,0:T(8,128)(2,1)} %copy-done.7), calls=%async_computation.3 | async-start | bytes 1572864 | tf_op jit(solution)/shard_map/all_to_all | solution.py:345
  117.4 0.7 slice.12
  118.1 11.0 %all-to-all-done.3.r_ref = bf16[16,192,128]{2,1,0:T(8,128)(2,1)S(1)} async-done(((bf16[16,192,128]{2,1,0:T(8,128)(2,1)}), bf16[16,192,128]{2,1,0:T(8,128)(2,1)S(1)}, u32[]{:S(2)}, u32[]{:S(2)}) %all-to-all-start.3) | async-done | bytes 786464 | tf_op jit(solution)/shard_map/all_to_all | solution.py:345
  129.1 0.9 copy-done.1
  130.0 0.4 expert_out.1
  130.4 0.0 copy-start.4
  130.5 0.9 copy-done.4
  131.4 12.1 %all_to_all.62.r_ref = bf16[8,64,128]{2,1,0:T(8,128)(2,1)S(1)} all-to-all(bf16[8,64,128]{2,1,0:T(8,128)(2,1)S(1)} %get-tuple-element.32), channel_id=1, replica_groups=mesh['eh'=8,'el'=8,'fsdp'=16] {'el'}, dimensions={0} | all-to-all | bytes 262144 | tf_op jit(solution)/shard_map/all_to_all | solution.py:345
  143.4 0.3 combine.1
  143.7 24.8 %all_to_all.63.r_ref = bf16[8,32,128]{2,1,0:T(8,128)(2,1)S(1)} all-to-all(bf16[8,32,128]{2,1,0:T(8,128)(2,1)S(1)} %combine.1), channel_id=1, replica_groups=mesh['eh'=8,'el'=8,'fsdp'=16] {'eh'}, dimensions={0} | all-to-all | bytes 131072 | tf_op jit(solution)/shard_map/all_to_all | solution.py:345
  168.5 0.0 copy-done.19
  168.5 0.6 resid.1
  169.1 25.5 %all_to_all.64.r_ref = bf16[8,32,128]{2,1,0:T(8,128)(2,1)S(1)} all-to-all(bf16[8,32,128]{2,1,0:T(8,128)(2,1)S(1)} %get-tuple-element.35), channel_id=1, replica_groups=mesh['eh'=8,'el'=8,'fsdp'=16] {'eh'}, dimensions={0} | all-to-all | bytes 131072 | tf_op jit(solution)/shard_map/all_to_all | solution.py:345
  194.6 0.2 redispatch.1
  194.8 12.9 %all_to_all.65.r_ref = bf16[8,64,128]{2,1,0:T(8,128)(2,1)S(1)} all-to-all(bf16[8,64,128]{2,1,0:T(8,128)(2,1)S(1)} %redispatch.1), channel_id=1, replica_groups=mesh['eh'=8,'el'=8,'fsdp'=16] {'el'}, dimensions={0} | all-to-all | bytes 262144 | tf_op jit(solution)/shard_map/all_to_all | solution.py:345
  207.7 0.9 delta_in.1
  208.7 0.0 copy-start.6
  208.7 0.9 copy-done.6
  209.6 0.7 copy-done.11
  210.2 3.6 %all-to-all-start.8 = ((bf16[16,192,128]{2,1,0:T(8,128)(2,1)}), bf16[16,192,128]{2,1,0:T(8,128)(2,1)S(1)}, u32[]{:S(2)}, u32[]{:S(2)}) async-start(bf16[16,192,128]{2,1,0:T(8,128)(2,1)} %copy-done.6), calls=%async_computation.8 | async-start | bytes 1572864 | tf_op jit(solution)/shard_map/all_to_all | solution.py:345
  213.9 1.1 copy-done.5
  215.0 0.9 copy-done.12
  215.9 0.4 grad_down.1.gd_ref
  216.3 0.0 copy-start.2
  216.3 0.7 copy-done.2
  217.1 9.6 %all-to-all-done.8.r_ref = bf16[16,192,128]{2,1,0:T(8,128)(2,1)S(1)} async-done(((bf16[16,192,128]{2,1,0:T(8,128)(2,1)}), bf16[16,192,128]{2,1,0:T(8,128)(2,1)S(1)}, u32[]{:S(2)}, u32[]{:S(2)}) %all-to-all-start.8) | async-done | bytes 786464 | tf_op jit(solution)/shard_map/all_to_all | solution.py:345
  226.6 1.0 copy-done.3
  227.6 0.9 copy-done.16
  228.5 0.9 copy-done.18
  229.4 0.4 delta.1
  229.8 0.0 copy-start
  229.8 1.2 copy-done
  231.0 0.6 copy-done.13
  231.7 4.4 %all-to-all-start.9 = ((bf16[16,480,128]{2,1,0:T(8,128)(2,1)}), bf16[16,480,128]{2,1,0:T(8,128)(2,1)}, u32[]{:S(2)}, u32[]{:S(2)}) async-start(bf16[16,480,128]{2,1,0:T(8,128)(2,1)} %copy-done), calls=%async_computation.9 | async-start | bytes 3932160 | tf_op jit(solution)/shard_map/all_to_all | solution.py:345
  236.1 0.0 copy-start.14
  236.1 24.2 %all-to-all-done.9.r_ref = bf16[16,480,128]{2,1,0:T(8,128)(2,1)} async-done(((bf16[16,480,128]{2,1,0:T(8,128)(2,1)}), bf16[16,480,128]{2,1,0:T(8,128)(2,1)}, u32[]{:S(2)}, u32[]{:S(2)}) %all-to-all-start.9) | async-done | bytes 1966112 | tf_op jit(solution)/shard_map/all_to_all | solution.py:345
  260.3 2.2 back.1
  262.5 13.4 %all_to_all.66.r_ref = bf16[8,64,128]{2,1,0:T(8,128)(2,1)S(1)} all-to-all(bf16[8,64,128]{2,1,0:T(8,128)(2,1)S(1)} %back.1), channel_id=1, replica_groups=mesh['eh'=8,'el'=8,'fsdp'=16] {'el'}, dimensions={0} | all-to-all | bytes 262144 | tf_op jit(solution)/shard_map/all_to_all | solution.py:345
  275.9 1.1 combine_back.1
  277.0 3.4 %all-to-all-start.11 = ((bf16[8,48,128]{2,1,0:T(8,128)(2,1)}), bf16[8,48,128]{2,1,0:T(8,128)(2,1)S(1)}, u32[]{:S(2)}, u32[]{:S(2)}) async-start(bf16[8,48,128]{2,1,0:T(8,128)(2,1)} %combine_back.1), calls=%async_computation.11 | async-start | bytes 196608 | tf_op jit(solution)/shard_map/all_to_all | solution.py:345
  280.4 1.3 grad_gate.1
  281.7 2.3 grad_down_out.1
  284.0 18.7 %all-to-all-done.11.r_ref = bf16[8,48,128]{2,1,0:T(8,128)(2,1)S(1)} async-done(((bf16[8,48,128]{2,1,0:T(8,128)(2,1)}), bf16[8,48,128]{2,1,0:T(8,128)(2,1)S(1)}, u32[]{:S(2)}, u32[]{:S(2)}) %all-to-all-start.11) | async-done | bytes 98336 | tf_op jit(solution)/shard_map/all_to_all | solution.py:345
  302.7 0.6 finish.1
  303.3 0.6 slice_bitcast_fusion
  (17 shorter events, 0.1 us)
Async XLA Ops:
  3.5 51.5 %all-to-all-start = ((bf16[8,48,128]{2,1,0:T(8,128)(2,1)}), bf16[8,48,128]{2,1,0:T(8,128)(2,1)S(1)}, u32[]{:S(2)}, u32[]{:S(2)}) async-start(bf16[8,48,128]{2,1,0:T(8,128)(2,1)} %broadcast_in_dim.19), calls=%async_computation | async-start | bytes 196608 | tf_op jit(solution)/shard_map/all_to_all | solution.py:345
  70.7 0.9 copy-start.8
  71.6 0.9 copy-start.9
  72.5 0.9 copy-start.10
  111.5 0.9 copy-start.7
  112.4 0.6 copy-start.15
  113.0 0.6 copy-start.17
  113.6 54.8 %copy-start.19 = (bf16[32,128]{1,0:T(8,128)(2,1)S(1)}, bf16[32,128]{1,0:T(8,128)(2,1)}, u32[]{:S(2)}) copy-start(bf16[32,128]{1,0:T(8,128)(2,1)} %t_ref.1) | copy-start | bytes 24580
  113.7 15.4 %all-to-all-start.3 = ((bf16[16,192,128]{2,1,0:T(8,128)(2,1)}), bf16[16,192,128]{2,1,0:T(8,128)(2,1)S(1)}, u32[]{:S(2)}, u32[]{:S(2)}) async-start(bf16[16,192,128]{2,1,0:T(8,128)(2,1)} %copy-done.7), calls=%async_computation.3 | async-start | bytes 1572864 | tf_op jit(solution)/shard_map/all_to_all | solution.py:345
  129.1 0.9 copy-start.1
  130.4 0.9 copy-start.4
  208.7 0.9 copy-start.6
  209.6 0.7 copy-start.11
  210.2 16.4 %all-to-all-start.8 = ((bf16[16,192,128]{2,1,0:T(8,128)(2,1)}), bf16[16,192,128]{2,1,0:T(8,128)(2,1)S(1)}, u32[]{:S(2)}, u32[]{:S(2)}) async-start(bf16[16,192,128]{2,1,0:T(8,128)(2,1)} %copy-done.6), calls=%async_computation.8 | async-start | bytes 1572864 | tf_op jit(solution)/shard_map/all_to_all | solution.py:345
  213.9 1.1 copy-start.5
  215.0 0.9 copy-start.12
  216.3 0.7 copy-start.2
  226.6 1.0 copy-start.3
  227.6 0.9 copy-start.16
  228.5 0.9 copy-start.18
  229.8 1.3 copy-start
  231.0 0.6 copy-start.13
  231.7 28.6 %all-to-all-start.9 = ((bf16[16,480,128]{2,1,0:T(8,128)(2,1)}), bf16[16,480,128]{2,1,0:T(8,128)(2,1)}, u32[]{:S(2)}, u32[]{:S(2)}) async-start(bf16[16,480,128]{2,1,0:T(8,128)(2,1)} %copy-done), calls=%async_computation.9 | async-start | bytes 3932160 | tf_op jit(solution)/shard_map/all_to_all | solution.py:345
  236.1 44.2 %copy-start.14 = (bf16[96,512]{1,0:T(8,128)(2,1)S(1)}, bf16[96,512]{1,0:T(8,128)(2,1)}, u32[]{:S(2)}) copy-start(bf16[96,512]{1,0:T(8,128)(2,1)} %copy-done.13) | copy-start | bytes 294916
  277.0 25.7 %all-to-all-start.11 = ((bf16[8,48,128]{2,1,0:T(8,128)(2,1)}), bf16[8,48,128]{2,1,0:T(8,128)(2,1)S(1)}, u32[]{:S(2)}, u32[]{:S(2)}) async-start(bf16[8,48,128]{2,1,0:T(8,128)(2,1)} %combine_back.1), calls=%async_computation.11 | async-start | bytes 196608 | tf_op jit(solution)/shard_map/all_to_all | solution.py:345

commit v2 on v1

--- a/solution.py
+++ b/solution.py
@@ -18,9 +18,11 @@
     return lax.dot_general(a, b, (((ca,), (cb,)), ((), ())), preferred_element_type=F4)
 
 
-def call(body, outs, *args, smem=(), flops=1e8, name=None):
+def call(body, outs, *args, smem=(), hbm=(), scratch=(), vmem_mib=16, name=None):
     specs = [
-        pl.BlockSpec(memory_space=pltpu.SMEM if i in smem else pltpu.VMEM)
+        pl.BlockSpec(
+            memory_space=pltpu.SMEM if i in smem else pltpu.HBM if i in hbm else pltpu.VMEM
+        )
         for i in range(len(args))
     ]
     nbytes = sum(a.size * a.dtype.itemsize for a in args)
@@ -30,9 +32,10 @@
         out_shape=shapes,
         in_specs=specs,
         out_specs=[pl.BlockSpec(memory_space=pltpu.VMEM) for _ in shapes],
-        compiler_params=pltpu.CompilerParams(vmem_limit_bytes=40 * 1024 * 1024),
+        scratch_shapes=list(scratch),
+        compiler_params=pltpu.CompilerParams(vmem_limit_bytes=vmem_mib * 1024 * 1024),
         cost_estimate=pl.CostEstimate(
-            flops=int(flops), bytes_accessed=int(nbytes), transcendentals=0
+            flops=100_000_000, bytes_accessed=int(nbytes), transcendentals=0
         ),
         name=name,
     )(*args)
@@ -82,6 +85,38 @@
     return jnp.concatenate(
         [x[i * rows : (i + 1) * rows] for i in range(x.shape[0] // rows)], axis=1
     )
+
+
+def first_body(base_ref, ids_in, weights_in, t_in, m_ref, ids_ref, weights_ref, t_ref, sem):
+    k, g = ids_ref.shape
+    pairs = ((ids_in, ids_ref), (weights_in, weights_ref), (t_in, t_ref))
+    copies = [pltpu.make_async_copy(a, b, sem.at[i]) for i, (a, b) in enumerate(pairs)]
+    for copy in copies:
+        copy.start()
+    for copy in copies:
+        copy.wait()
+    w = weights_ref[...]
+    hi = w.astype(BF)
+    rest = w - hi.astype(F4)
+    mid = rest.astype(BF)
+    low = (rest - mid.astype(F4)).astype(BF)
+    row = lax.broadcasted_iota(jnp.int32, (g, LANES), 0)
+    col = lane((g, LANES))
+    meta = jnp.zeros((k, LANES), F4)
+    for i, part in enumerate((ids_ref[...].astype(F4).astype(BF), hi, mid, low)):
+        move = jnp.where(col == row + i * g, 1.0, 0.0).astype(BF)
+        meta = meta + dot(part, move)
+    tail = jnp.concatenate([meta, jnp.zeros_like(meta)], axis=0).astype(BF)
+    message = jnp.concatenate([t_ref[...], tail], axis=0)
+    for i in range(m_ref.shape[0]):
+        m_ref[i] = message
+
+
+def weights_body(wg_ref, wu_ref, wd_ref, wgu_ref, wd_out_ref):
+    fs = wg_ref.shape[0]
+    wgu_ref[:fs] = wg_ref[...]
+    wgu_ref[fs:] = wu_ref[...]
+    wd_out_ref[...] = wd_ref[...]
 
 
 def dispatch_body(base_ref, r_ref, m_ref, p_ref, ids_ref):
@@ -132,9 +167,9 @@
         m_ref[e] = jnp.concatenate([rows[: CAP * h], tile], axis=0).astype(BF)
 
 
-def expert_in_body(r_ref, wg_ref, wu_ref, wd_ref, f_ref, w_ref):
+def expert_in_body(r_ref, wd_ref, f_ref, w_ref):
     l, h = r_ref.shape[0], r_ref.shape[1] // 8
-    fs = wg_ref.shape[0]
+    fs = wd_ref.shape[0]
     rows = []
     for e in range(l):
         v = r_ref[e].astype(F4)
@@ -142,24 +177,20 @@
         w_ref[e] = join3(v[CAP * h :], 8)
     x = jnp.concatenate(rows, axis=0).astype(BF)
     for d in range(f_ref.shape[0]):
-        part = pl.ds(d * LANES, LANES)
-        f_ref[d, 0:fs] = wg_ref[:, part]
-        f_ref[d, fs : 2 * fs] = wu_ref[:, part]
-        f_ref[d, 2 * fs : 3 * fs] = wd_ref[:, part]
-        f_ref[d, 3 * fs :] = x
-
-
-def hidden_body(r_ref, wg_ref, wu_ref, gate_ref, up_ref, f_ref):
-    n, fs = r_ref.shape[0], wg_ref.shape[0]
+        f_ref[d, :fs] = wd_ref[:, d * LANES : (d + 1) * LANES]
+        f_ref[d, fs:] = x
+
+
+def hidden_body(r_ref, wgu_ref, gate_ref, up_ref, wd_ref, f_ref):
+    n, fs = r_ref.shape[0], gate_ref.shape[0]
     slots = gate_ref.shape[1]
-    held = r_ref.shape[1] - 3 * fs
+    held = r_ref.shape[1] - fs
     pad = jnp.zeros((slots - held, 2 * LANES), BF)
     total = jnp.zeros((2 * fs, slots), F4)
     for i in range(n // 2):
-        x = jnp.concatenate([r_ref[2 * i, 3 * fs :], r_ref[2 * i + 1, 3 * fs :]], axis=1)
+        x = jnp.concatenate([r_ref[2 * i, fs:], r_ref[2 * i + 1, fs:]], axis=1)
         x = jnp.concatenate([x, pad], axis=0)
-        part = pl.ds(2 * i * LANES, 2 * LANES)
-        w = jnp.concatenate([wg_ref[:, part], wu_ref[:, part]], axis=0)
+        w = wgu_ref[:, 2 * i * LANES : 2 * (i + 1) * LANES]
         total = total + dot(w, x, 1, 1)
     gate, up = total[:fs], total[fs:]
     gate_ref[...] = gate
@@ -168,6 +199,7 @@
     message = blocks_to_rows(hidden)
     for d in range(n):
         f_ref[d] = message
+        wd_ref[d * fs : (d + 1) * fs] = r_ref[d, :fs]
 
 
 def expert_out_body(r_ref, wd_ref, w_ref, out_ref, h_ref, m_ref):
@@ -210,10 +242,10 @@
         m_ref[e] = dot(p_ref[e], x).astype(BF)
 
 
-def delta_in_body(r_ref, w_ref, out_ref, wd_ref, f_ref, s_ref):
+def delta_in_body(r_ref, w_ref, out_ref, wd_ref, h_ref, f_ref, g_ref):
     l, h = w_ref.shape[0], w_ref.shape[1]
     n, fs = f_ref.shape[0], f_ref.shape[1] // 4
-    slots = s_ref.shape[0]
+    slots = h_ref.shape[1]
     rows, tiles = [], []
     for e in range(l):
         resid = r_ref[e].astype(F4)[: CAP * h]
@@ -223,7 +255,6 @@
         rows.append(scale_rows(resid, w_ref[e], h))
     rows.append(jnp.zeros((slots - l * CAP * h, LANES), F4))
     scaled = jnp.concatenate(rows, axis=0).astype(BF)
-    s_ref[...] = scaled
     half = l // 2
     packed = roll(jnp.concatenate(tiles[:half], axis=0), 64) + roll(
         jnp.concatenate(tiles[half:], axis=0), 88
@@ -234,18 +265,10 @@
         message = blocks_to_rows(part)
         last = message[3 * fs :] + packed
         f_ref[d] = jnp.concatenate([message[: 3 * fs], last], axis=0).astype(BF)
-
-
-def grad_down_body(h_ref, s_ref, g_ref):
-    n, fs = g_ref.shape[0], g_ref.shape[1] // 2
-    for d in range(n):
-        grad = dot(h_ref[d * fs : (d + 1) * fs], s_ref[...])
-        hi = grad.astype(BF)
-        g_ref[d, :fs] = hi
-        g_ref[d, fs:] = (grad - hi.astype(F4)).astype(BF)
-
-
-def delta_body(r_ref, gate_ref, up_ref, gd_ref, f_ref, dgu_ref, dot_ref):
+        g_ref[d] = dot(h_ref[d * fs : (d + 1) * fs], scaled).astype(BF)
+
+
+def delta_body(r_ref, gate_ref, up_ref, wgu_ref, gd_ref, f_ref, dgu_ref, dot_ref):
     n, fs = f_ref.shape[0], gate_ref.shape[0]
     l, h = dot_ref.shape[0], dot_ref.shape[1]
     total = r_ref[0].astype(F4)
@@ -265,45 +288,42 @@
     dup = (dh * gate * s).astype(BF)
     dgu = jnp.concatenate([dgate, dup], axis=0)
     dgu_ref[...] = dgu
-    message = blocks_to_rows(dgu)
-    for d in range(n):
-        f_ref[d, : 8 * fs] = message
-        f_ref[d, 8 * fs :] = gd_ref[d]
-
-
-def back_body(r_ref, wgu_ref, dot_ref, m_ref):
-    n, fs = r_ref.shape[0], r_ref.shape[1] // 10
+    held = CAP * h * l
+    for i in range(n // 2):
+        back = dot(dgu, wgu_ref[:, 2 * i * LANES : 2 * (i + 1) * LANES], 0, 0)
+        back = back[:held].astype(BF)
+        for d in (2 * i, 2 * i + 1):
+            own = (d - 2 * i) * LANES
+            f_ref[d, :fs] = gd_ref[d]
+            f_ref[d, fs:] = back[:, own : own + LANES]
+
+
+def back_body(r_ref, dot_ref, m_ref, gd_ref):
     l, h = dot_ref.shape[0], dot_ref.shape[1]
-    dgu = jnp.concatenate(
-        [rows_to_blocks(r_ref[i, : 8 * fs], 2 * fs) for i in range(n)], axis=0
-    )
-    back = dot(dgu, wgu_ref[...], 0, 0)
-    for e in range(l):
-        rows = back[e * CAP * h : (e + 1) * CAP * h]
+    fs = r_ref.shape[1] - CAP * h * l
+    for e in range(l):
+        part = pl.ds(fs + e * CAP * h, CAP * h)
+        rows = r_ref[0, part].astype(F4)
+        for i in range(1, r_ref.shape[0]):
+            rows = rows + r_ref[i, part].astype(F4)
         m_ref[e] = jnp.concatenate([rows, split3(dot_ref[e], 8)], axis=0).astype(BF)
-
-
-def grad_gate_body(r_ref, dgu_ref, gg_ref, gu_ref):
-    n, fs = r_ref.shape[0], gg_ref.shape[0]
+    for i in range(r_ref.shape[0]):
+        gd_ref[:, i * LANES : (i + 1) * LANES] = r_ref[i, :fs].astype(F4)
+
+
+def grads_body(tick_ref, x_ref, dgu_ref, gg_ref, gu_ref):
+    n, fs = x_ref.shape[0], gg_ref.shape[0]
     dgu = dgu_ref[...]
-    slots = dgu.shape[1]
-    pad = jnp.zeros((slots - r_ref.shape[1] + 3 * fs, 2 * LANES), BF)
+    pad = jnp.zeros((dgu.shape[1] - x_ref.shape[1] + fs, 2 * LANES), BF)
     for i in range(n // 2):
-        x = jnp.concatenate([r_ref[2 * i, 3 * fs :], r_ref[2 * i + 1, 3 * fs :]], axis=1)
+        x = jnp.concatenate([x_ref[2 * i, fs:], x_ref[2 * i + 1, fs:]], axis=1)
         grad = dot(dgu, jnp.concatenate([x, pad], axis=0))
         part = pl.ds(2 * i * LANES, 2 * LANES)
         gg_ref[:, part] = grad[:fs]
         gu_ref[:, part] = grad[fs:]
 
 
-def grad_down_out_body(r_ref, gd_ref):
-    fs = gd_ref.shape[0]
-    for i in range(r_ref.shape[0]):
-        hi, mid = r_ref[i, 8 * fs : 9 * fs], r_ref[i, 9 * fs :]
-        gd_ref[:, i * LANES : (i + 1) * LANES] = hi.astype(F4) + mid.astype(F4)
-
-
-def combine_back_body(base_ref, r_ref, p_ref, ids_ref, m_ref):
+def combine_back_body(base_ref, r_ref, p_ref, ids_ref, m_ref, tick_ref):
     l, hosts = r_ref.shape[0], m_ref.shape[0]
     h = hosts
     g = 32
@@ -312,6 +332,7 @@
     p = jnp.concatenate([p_ref[i] for i in range(l)], axis=0)
     y = dot(p, x, 0, 0)
     ids = ids_ref[...]
+    tick_ref[...] = ids[:, :LANES]
     routes = jnp.zeros(ids.shape, F4)
     for e in range(l):
         tile = join3(r_ref[e].astype(F4)[CAP * h :], 8)
@@ -338,7 +359,7 @@
         total = total + r_ref[i].astype(F4)
     rows = t_ref.shape[0]
     t_ref[...] = total[:rows].astype(BF)
-    g_ref[...] = join3(total[rows : rows + 8], rows)
+    g_ref[...] = join3(total[rows : rows + 8], rows)[:, :rows]
 
 
 def exchange(x, axis):
@@ -357,14 +378,19 @@
     held, slots = CAP * h * l, 8 * h * l
     base = (lax.axis_index("eh") * l).astype(jnp.int32).reshape(1)
 
-    weights = route_weights.T
-    hi = lax.reduce_precision(weights, 8, 7)
-    mid = lax.reduce_precision(weights - hi, 8, 7)
-    low = weights - hi - mid
-    meta = jnp.concatenate([expert_ids.T.astype(F4), hi, mid, low], axis=1).astype(BF)
-    first = jnp.concatenate([tokens, meta, jnp.zeros((8, LANES), BF)], axis=0)
-    first = jnp.broadcast_to(first[None], (h,) + first.shape)
-    got = exchange(first, "eh")
+    (message,) = call(
+        first_body, [((h, g + 16, df), BF)],
+        base, expert_ids.T, route_weights.T, tokens, smem=(0,), hbm=(1, 2, 3),
+        scratch=(
+            pltpu.VMEM((k, g), jnp.int32), pltpu.VMEM((k, g), F4), pltpu.VMEM((g, df), BF),
+            pltpu.SemaphoreType.DMA((3,)),
+        ),
+        vmem_mib=60, name="first",
+    )
+    got = exchange(message, "eh")
+    wgu, wd = call(
+        weights_body, [((2 * fs, d), BF), ((fs, d), BF)], wg, wu, wd, name="weights"
+    )
     message, place, ids = call(
         dispatch_body,
         [((l, 8 * h, df), BF), ((l, 8 * h, h * g), BF), ((8, h * g), F4)],
@@ -373,17 +399,16 @@
     got = exchange(message, "el")
     message, w_tile = call(
         expert_in_body,
-        [((n, 3 * fs + held, df), BF), ((l, h, LANES), F4)],
-        got, wg, wu, wd, name="expert_in",
+        [((n, fs + held, df), BF), ((l, h, LANES), F4)],
+        got, wd, name="expert_in",
     )
     rows = exchange(message, "fsdp")
-    gate, up, message = call(
+    packed = (n, fs * slots // LANES, LANES)
+    gate, up, wd_f, message = call(
         hidden_body,
-        [((fs, slots), F4), ((fs, slots), F4), ((n, fs * slots // LANES, LANES), BF)],
-        rows, wg, wu, name="hidden",
-    )
-    wgu_f = rows[:, : 2 * fs].reshape(n * 2 * fs, df)
-    wd_f = rows[:, 2 * fs : 3 * fs].reshape(n * fs, df)
+        [((fs, slots), F4), ((fs, slots), F4), ((n * fs, df), BF), (packed, BF)],
+        rows, wgu, name="hidden",
+    )
     got = exchange(message, "fsdp")
     out, hidden, message = call(
         expert_out_body,
@@ -401,39 +426,37 @@
         redispatch_body, [((l, 8 * h, df), BF)], got, place, name="redispatch"
     )
     got = exchange(message, "el")
-    message, scaled = call(
+    message, down = call(
         delta_in_body,
-        [((n, fs * slots // LANES, LANES), BF), ((slots, df), BF)],
-        got, w_tile, out, wd_f, name="delta_in",
+        [(packed, BF), ((n, fs, df), BF)],
+        got, w_tile, out, wd_f, hidden, name="delta_in",
     )
     got = exchange(message, "fsdp")
-    (grad_down_parts,) = call(
-        grad_down_body, [((n, 2 * fs, df), BF)], hidden, scaled, name="grad_down"
-    )
     message, dgu, dots = call(
         delta_body,
-        [((n, 10 * fs, LANES), BF), ((2 * fs, slots), BF), ((l, h, LANES), F4)],
-        got, gate, up, grad_down_parts, name="delta",
-    )
-    deltas = exchange(message, "fsdp")
+        [((n, fs + held, df), BF), ((2 * fs, slots), BF), ((l, h, LANES), F4)],
+        got, gate, up, wgu, down, name="delta",
+    )
+    got = exchange(message, "fsdp")
+    message, grad_down = call(
+        back_body, [((l, 8 * h, df), BF), ((fs, d), F4)], got, dots, name="back"
+    )
+    got = exchange(message, "el")
+    message, tick = call(
+        combine_back_body,
+        [((h, g + 16, df), BF), ((8, LANES), F4)],
+        base, got, place, ids, smem=(0,), name="combine_back",
+    )
+    got = exchange(message, "eh")
     grad_gate, grad_up = call(
-        grad_gate_body, [((fs, d), F4), ((fs, d), F4)], rows, dgu, name="grad_gate"
-    )
-    (message,) = call(
-        back_body, [((l, 8 * h, df), BF)], deltas, wgu_f, dots, name="back"
-    )
-    got = exchange(message, "el")
-    (grad_down,) = call(grad_down_out_body, [((fs, d), F4)], deltas, name="grad_down_out")
-    (message,) = call(
-        combine_back_body, [((h, g + 16, df), BF)],
-        base, got, place, ids, smem=(0,), name="combine_back",
-    )
-    got = exchange(message, "eh")
+        grads_body, [((fs, d), F4)] * 2, tick, rows, dgu, name="grads"
+    )
     grad_tokens, grad_route = call(
-        finish_body, [((g, df), BF), ((8, LANES), F4)], got, name="finish"
-    )
-    grad_route = grad_route[:, :g].T
-    return (layer_out, grad_tokens, grad_route, grad_gate[None], grad_up[None], grad_down[None])
+        finish_body, [((g, df), BF), ((8, g), F4)], got, name="finish"
+    )
+    return (
+        layer_out, grad_tokens, grad_route.T, grad_gate[None], grad_up[None], grad_down[None]
+    )
 
 
 def solution(mesh):

time: 309 us -> 287 us (0.929)
  blocking collectives: 141 us -> 230 us
  waiting for transfers between devices: 86 us -> 24 us
  starting transfers between devices: 44 us -> 12.9 us
  local copies, waits for them, and re-layouts: 17.8 us -> 2.79 us
    all_to_all x7 -> x10, blocking collectives: 141 us -> 230 us  [exchange(): return lax.all_to_all(x, axis, split_axis=0, concat_axis=0, tiled=True)]
    all_to_all x5 -> x2, waiting for transfers between devices: 86 us -> 24 us  [exchange(): return lax.all_to_all(x, axis, split_axis=0, concat_axis=0, tiled=True)]
    all_to_all x5 -> x2, starting transfers between devices: 44 us -> 12.9 us  [exchange(): return lax.all_to_all(x, axis, split_axis=0, concat_axis=0, tiled=True)]
    unnamed x40 -> x8, local copies, waits for them, and re-layouts: 15.7 us -> 2.79 us
  transfers between devices with their start and end apart: 5 -> 2, of which waited for: 5 -> 2; matrix products, arithmetic and copies ran while one was open for 0% -> 0% of each run, Pallas kernels for 1% -> 0%
where the time goes in v2:
time: 287 us; the launch traced here: 282 us
  blocking collectives  230 us (80%)
  waiting for transfers between devices  24 us (8%)
  starting transfers between devices  12.9 us (4%)
  Pallas kernels  11.4 us (4%)
    all_to_all x10, blocking collectives, exchange(): return lax.all_to_all(x, axis, split_axis=0, concat_axis=0, tiled=True)  230 us
    all_to_all x2, waiting for transfers between devices, exchange(): return lax.all_to_all(x, axis, split_axis=0, concat_axis=0, tiled=True)  24 us
    all_to_all x2, starting transfers between devices, exchange(): return lax.all_to_all(x, axis, split_axis=0, concat_axis=0, tiled=True)  12.9 us
    pallas_call x15, Pallas kernels, call(): pl.pallas_call(body, out_shape=shapes, in_specs=specs, out_specs=[pl.Bloc...  11.4 us
  transfers between devices with their start and end apart: 2, of which 2 were waited for; matrix products, arithmetic and copies ran while one was open for 0% of the time, Pallas kernels for 0%

profile of v2, /device:TPU:1, one launch (start us, length us, event | category | flops | bytes accessed | tf_op | source)
XLA Modules:
  0.0 282.3 jit_solution(1196798060468729895)
XLA Ops:
  0.6 1.5 first.1
  2.2 51.5 %all_to_all.60.r_ref = bf16[8,48,128]{2,1,0:T(8,128)(2,1)S(1)} all-to-all(bf16[8,48,128]{2,1,0:T(8,128)(2,1)} %first.1), channel_id=1, replica_groups=mesh['eh'=8,'el'=8,'fsdp'=16] {'eh'}, dimensions={0} | all-to-all | bytes 196608 | tf_op jit(solution)/shard_map/all_to_all | solution.py:366
  53.6 1.1 dispatch.1
  54.8 9.6 %all-to-all-start.1 = ((bf16[8,64,128]{2,1,0:T(8,128)(2,1)}), bf16[8,64,128]{2,1,0:T(8,128)(2,1)S(1)}, u32[]{:S(2)}, u32[]{:S(2)}) async-start(bf16[8,64,128]{2,1,0:T(8,128)(2,1)} %get-tuple-element.35), calls=%async_computation.1 | async-start | bytes 262144 | tf_op jit(solution)/shard_map/all_to_all | solution.py:366
  64.3 0.0 copy-start
  64.3 0.9 copy-done
  65.3 0.0 copy-start.1
  65.3 0.9 copy-done.1
  66.2 0.0 copy-start.2
  66.2 0.9 copy-done.2
  67.2 3.0 %all-to-all-done.1.r_ref = bf16[8,64,128]{2,1,0:T(8,128)(2,1)S(1)} async-done(((bf16[8,64,128]{2,1,0:T(8,128)(2,1)}), bf16[8,64,128]{2,1,0:T(8,128)(2,1)S(1)}, u32[]{:S(2)}, u32[]{:S(2)}) %all-to-all-start.1) | async-done | bytes 131104 | tf_op jit(solution)/shard_map/all_to_all | solution.py:366
  70.2 0.3 expert_in.1
  70.4 32.1 %all_to_all.61.r_ref.x_ref = bf16[16,496,128]{2,1,0:T(8,128)(2,1)S(1)} all-to-all(bf16[16,496,128]{2,1,0:T(8,128)(2,1)S(1)} %get-tuple-element.37), channel_id=1, replica_groups=mesh['eh'=8,'el'=8,'fsdp'=16] {'fsdp'}, dimensions={0} | all-to-all | bytes 4063232 | tf_op jit(solution)/shard_map/all_to_all | solution.py:366
  102.5 0.7 hidden.1
  103.3 0.0 copy-start.3
  103.3 15.9 %all_to_all.62.r_ref = bf16[16,192,128]{2,1,0:T(8,128)(2,1)S(1)} all-to-all(bf16[16,192,128]{2,1,0:T(8,128)(2,1)S(1)} %get-tuple-element.39), channel_id=1, replica_groups=mesh['eh'=8,'el'=8,'fsdp'=16] {'fsdp'}, dimensions={0} | all-to-all | bytes 1572864 | tf_op jit(solution)/shard_map/all_to_all | solution.py:366
  119.2 0.4 expert_out.1
  119.6 11.7 %all_to_all.63.r_ref = bf16[8,64,128]{2,1,0:T(8,128)(2,1)S(1)} all-to-all(bf16[8,64,128]{2,1,0:T(8,128)(2,1)S(1)} %get-tuple-element.42), channel_id=1, replica_groups=mesh['eh'=8,'el'=8,'fsdp'=16] {'el'}, dimensions={0} | all-to-all | bytes 262144 | tf_op jit(solution)/shard_map/all_to_all | solution.py:366
  131.3 0.3 combine.1
  131.6 24.8 %all_to_all.64.r_ref = bf16[8,32,128]{2,1,0:T(8,128)(2,1)S(1)} all-to-all(bf16[8,32,128]{2,1,0:T(8,128)(2,1)S(1)} %combine.1), channel_id=1, replica_groups=mesh['eh'=8,'el'=8,'fsdp'=16] {'eh'}, dimensions={0} | all-to-all | bytes 131072 | tf_op jit(solution)/shard_map/all_to_all | solution.py:366
  156.4 0.0 copy-done.3
  156.4 0.6 resid.1
  157.0 25.7 %all_to_all.65.r_ref = bf16[8,32,128]{2,1,0:T(8,128)(2,1)S(1)} all-to-all(bf16[8,32,128]{2,1,0:T(8,128)(2,1)S(1)} %get-tuple-element.45), channel_id=1, replica_groups=mesh['eh'=8,'el'=8,'fsdp'=16] {'eh'}, dimensions={0} | all-to-all | bytes 131072 | tf_op jit(solution)/shard_map/all_to_all | solution.py:366
  182.7 0.2 redispatch.1
  183.0 12.6 %all_to_all.66.r_ref = bf16[8,64,128]{2,1,0:T(8,128)(2,1)S(1)} all-to-all(bf16[8,64,128]{2,1,0:T(8,128)(2,1)S(1)} %redispatch.1), channel_id=1, replica_groups=mesh['eh'=8,'el'=8,'fsdp'=16] {'el'}, dimensions={0} | all-to-all | bytes 262144 | tf_op jit(solution)/shard_map/all_to_all | solution.py:366
  195.6 1.3 delta_in.1
  196.9 15.6 %all_to_all.67.r_ref = bf16[16,192,128]{2,1,0:T(8,128)(2,1)S(1)} all-to-all(bf16[16,192,128]{2,1,0:T(8,128)(2,1)S(1)} %get-tuple-element.48), channel_id=1, replica_groups=mesh['eh'=8,'el'=8,'fsdp'=16] {'fsdp'}, dimensions={0} | all-to-all | bytes 1572864 | tf_op jit(solution)/shard_map/all_to_all | solution.py:366
  212.5 0.8 delta.1
  213.3 28.1 %all_to_all.68.r_ref = bf16[16,496,128]{2,1,0:T(8,128)(2,1)S(1)} all-to-all(bf16[16,496,128]{2,1,0:T(8,128)(2,1)S(1)} %get-tuple-element.52), channel_id=1, replica_groups=mesh['eh'=8,'el'=8,'fsdp'=16] {'fsdp'}, dimensions={0} | all-to-all | bytes 4063232 | tf_op jit(solution)/shard_map/all_to_all | solution.py:366
  241.3 1.0 back.1
  242.4 12.5 %all_to_all.69.r_ref = bf16[8,64,128]{2,1,0:T(8,128)(2,1)S(1)} all-to-all(bf16[8,64,128]{2,1,0:T(8,128)(2,1)S(1)} %get-tuple-element.54), channel_id=1, replica_groups=mesh['eh'=8,'el'=8,'fsdp'=16] {'el'}, dimensions={0} | all-to-all | bytes 262144 | tf_op jit(solution)/shard_map/all_to_all | solution.py:366
  254.8 1.1 combine_back.1
  255.9 3.4 %all-to-all-start.11 = ((bf16[8,48,128]{2,1,0:T(8,128)(2,1)}), bf16[8,48,128]{2,1,0:T(8,128)(2,1)S(1)}, u32[]{:S(2)}, u32[]{:S(2)}) async-start(bf16[8,48,128]{2,1,0:T(8,128)(2,1)} %get-tuple-element.56), calls=%async_computation.11 | async-start | bytes 196608 | tf_op jit(solution)/shard_map/all_to_all | solution.py:366
  259.3 1.3 grads.1
  260.6 21.0 %all-to-all-done.11.r_ref = bf16[8,48,128]{2,1,0:T(8,128)(2,1)S(1)} async-done(((bf16[8,48,128]{2,1,0:T(8,128)(2,1)}), bf16[8,48,128]{2,1,0:T(8,128)(2,1)S(1)}, u32[]{:S(2)}, u32[]{:S(2)}) %all-to-all-start.11) | async-done | bytes 98336 | tf_op jit(solution)/shard_map/all_to_all | solution.py:366
  281.6 0.7 finish.1
  (1 shorter events, 0.0 us)
Async XLA Ops:
  54.8 15.4 %all-to-all-start.1 = ((bf16[8,64,128]{2,1,0:T(8,128)(2,1)}), bf16[8,64,128]{2,1,0:T(8,128)(2,1)S(1)}, u32[]{:S(2)}, u32[]{:S(2)}) async-start(bf16[8,64,128]{2,1,0:T(8,128)(2,1)} %get-tuple-element.35), calls=%async_computation.1 | async-start | bytes 262144 | tf_op jit(solution)/shard_map/all_to_all | solution.py:366
  64.3 0.9 copy-start
  65.3 0.9 copy-start.1
  66.2 0.9 copy-start.2
  103.3 53.1 %copy-start.3 = (bf16[32,128]{1,0:T(8,128)(2,1)S(1)}, bf16[32,128]{1,0:T(8,128)(2,1)}, u32[]{:S(2)}) copy-start(bf16[32,128]{1,0:T(8,128)(2,1)} %t_ref.1) | copy-start | bytes 24580
  255.9 25.7 %all-to-all-start.11 = ((bf16[8,48,128]{2,1,0:T(8,128)(2,1)}), bf16[8,48,128]{2,1,0:T(8,128)(2,1)S(1)}, u32[]{:S(2)}, u32[]{:S(2)}) async-start(bf16[8,48,128]{2,1,0:T(8,128)(2,1)} %get-tuple-element.56), calls=%async_computation.11 | async-start | bytes 196608 | tf_op jit(solution)/shard_map/all_to_all | solution.py:366

commit v3 on v2

--- a/solution.py
+++ b/solution.py
@@ -10,8 +10,10 @@
 BF = jnp.bfloat16
 F4 = jnp.float32
 LANES = 128
-HI = 8
+NEAR = 4
 CAP = 7
+ROWS = 8 * NEAR
+HELD = CAP * NEAR
 
 
 def dot(a, b, ca=1, cb=0):
@@ -61,18 +63,52 @@
     return x + roll(x, -step) + roll(x, -2 * step)
 
 
-def column_tile(column, h):
-    at = lane((h, LANES))
-    tile = jnp.zeros((h, LANES), F4)
-    for c in range(CAP):
-        tile = jnp.where(at == c, column[c * h : (c + 1) * h], tile)
-    return tile
-
-
-def scale_rows(rows, tile, h):
-    return jnp.concatenate(
-        [rows[c * h : (c + 1) * h] * tile[:, c : c + 1] for c in range(CAP)], axis=0
-    )
+def index(shape):
+    return lax.broadcasted_iota(jnp.int32, shape, 0), lane(shape)
+
+
+def onehot(hit):
+    return jnp.where(hit, 1.0, 0.0).astype(BF)
+
+
+def to_slots():
+    i, j = index((2 * HELD, 2 * ROWS))
+    return onehot(j == i // HELD * ROWS + i % HELD)
+
+
+def to_message():
+    i, j = index((2 * ROWS, 2 * HELD))
+    return onehot((j == i // ROWS * HELD + i % ROWS) & (i % ROWS < HELD))
+
+
+def scalar_rows():
+    i, j = index((2 * HELD, 2 * ROWS))
+    return onehot(j == i // HELD * ROWS + HELD + i % HELD % NEAR)
+
+
+def scalars_to_tile():
+    i, j = index((2 * NEAR, 2 * HELD))
+    return onehot((j // HELD == i // NEAR) & (j % HELD % NEAR == i % NEAR))
+
+
+def tile_to_message():
+    i, j = index((2 * ROWS, 2 * NEAR))
+    return onehot((i % ROWS >= HELD) & (j == i // ROWS * NEAR + i % ROWS - HELD))
+
+
+def spread(column, held):
+    i, j = index((column.shape[0], LANES))
+    return split3(jnp.where(j == i % held // NEAR, column, 0.0), 8).astype(BF)
+
+
+def gathered_column(rows, held):
+    i, j = index(rows.shape)
+    mine = (j % 8 == i % held // NEAR) & (j < 24)
+    return jnp.sum(jnp.where(mine, rows, 0.0), axis=1, keepdims=True)
+
+
+def pair(ref, p):
+    return jnp.concatenate([ref[2 * p], ref[2 * p + 1]], axis=0)
 
 
 def blocks_to_rows(x):
@@ -120,61 +156,53 @@
 
 
 def dispatch_body(base_ref, r_ref, m_ref, p_ref, ids_ref):
-    h, l = r_ref.shape[0], m_ref.shape[0]
-    g = 32
-    width = h * g
-    per = LANES // g
+    l, h = r_ref.shape[0], m_ref.shape[0]
+    g = LANES // l
     at = lane((8, LANES))
-    metas = [r_ref[i].astype(F4)[g : g + 8] for i in range(h)]
+    metas = [r_ref[i].astype(F4)[g : g + 8] for i in range(l)]
 
     def gathered(parts, start):
-        out = []
-        for q in range(h // per):
-            acc = jnp.zeros((8, LANES), F4)
-            for i in range(per):
-                moved = roll(parts[q * per + i], i * g - start)
-                acc = jnp.where(at // g == i, moved, acc)
-            out.append(acc)
-        return jnp.concatenate(out, axis=1)
+        out = jnp.zeros((8, LANES), F4)
+        for i in range(l):
+            out = jnp.where(at // g == i, roll(parts[i], i * g - start), out)
+        return out
 
     ids = gathered(metas, 0)
     weights = gathered([join3(m, g) for m in metas], g)
     ids_ref[...] = ids
-    mine = (lax.broadcasted_iota(jnp.int32, (l, width), 0) + base_ref[0]).astype(F4)
-    named = jnp.zeros((l, width), F4)
-    weight_at = jnp.zeros((l, width), F4)
+    mine = (lax.broadcasted_iota(jnp.int32, (h, LANES), 0) * l + base_ref[0]).astype(F4)
+    named = jnp.zeros((h, LANES), F4)
+    weight_at = jnp.zeros((h, LANES), F4)
     for k in range(8):
         hit = ids[k : k + 1] == mine
         named = named + jnp.where(hit, 1.0, 0.0)
         weight_at = weight_at + jnp.where(hit, weights[k : k + 1], 0.0)
-    row = lax.broadcasted_iota(jnp.int32, (width, width), 0)
-    col = lane((width, width))
-    before = jnp.where((row // g == col // g) & (row < col), 1.0, 0.0).astype(BF)
-    rank = dot(named.astype(BF), before)
+    row, col = index((LANES, LANES))
+    rank = dot(named.astype(BF), onehot((row // g == col // g) & (row < col)))
     rank = jnp.where(named > 0.0, rank, -1.0)
-    block = lane((h, width)) // g == lax.broadcasted_iota(jnp.int32, (h, width), 0)
-    x = jnp.concatenate([r_ref[i][:g] for i in range(h)], axis=0)
-    for e in range(l):
-        own = jnp.broadcast_to(rank[e : e + 1], (h, width))
-        place = jnp.concatenate(
-            [jnp.where(block & (own == float(c)), 1.0, 0.0) for c in range(8)], axis=0
-        )
+    x = jnp.concatenate([r_ref[i][:g] for i in range(l)], axis=0)
+    i, j = index((ROWS, LANES))
+    own = (j // g == i % NEAR) & (i < HELD)
+    slot = (i // NEAR).astype(F4)
+    i, j = index((ROWS, ROWS))
+    down = onehot((i >= HELD) & (j % NEAR == i - HELD) & (j < HELD))
+    for e in range(h):
+        place = jnp.where(own & (rank[e : e + 1] == slot), 1.0, 0.0)
         column = jnp.sum(place * weight_at[e : e + 1], axis=1, keepdims=True)
         place = place.astype(BF)
         p_ref[e] = place
-        rows = dot(place, x)
-        tile = split3(column_tile(column, h), 8)
-        m_ref[e] = jnp.concatenate([rows[: CAP * h], tile], axis=0).astype(BF)
+        m_ref[e] = (dot(place, x) + dot(down, spread(column, ROWS))).astype(BF)
 
 
 def expert_in_body(r_ref, wd_ref, f_ref, w_ref):
-    l, h = r_ref.shape[0], r_ref.shape[1] // 8
     fs = wd_ref.shape[0]
+    slots, scalars = to_slots(), scalar_rows()
     rows = []
-    for e in range(l):
-        v = r_ref[e].astype(F4)
-        rows.append(v[: CAP * h])
-        w_ref[e] = join3(v[CAP * h :], 8)
+    for p in range(r_ref.shape[0] // 2):
+        v = pair(r_ref, p)
+        rows.append(dot(slots, v))
+        column = gathered_column(dot(scalars, v), HELD)
+        w_ref[p] = jnp.broadcast_to(column, (2 * HELD, LANES))
     x = jnp.concatenate(rows, axis=0).astype(BF)
     for d in range(f_ref.shape[0]):
         f_ref[d, :fs] = wd_ref[:, d * LANES : (d + 1) * LANES]
@@ -204,58 +232,58 @@
 
 def expert_out_body(r_ref, wd_ref, w_ref, out_ref, h_ref, m_ref):
     n, fs = r_ref.shape[0], r_ref.shape[1] // 4
-    l, h = w_ref.shape[0], w_ref.shape[1]
     hidden = jnp.concatenate([rows_to_blocks(r_ref[i], fs) for i in range(n)], axis=0)
     h_ref[...] = hidden
     out = dot(hidden, wd_ref[...], 0, 0)
     out_ref[...] = out
-    for e in range(l):
-        rows = out[e * CAP * h : (e + 1) * CAP * h]
-        rows = scale_rows(rows, w_ref[e], h)
-        m_ref[e] = jnp.concatenate([rows, jnp.zeros((h, LANES), F4)], axis=0).astype(BF)
-
-
-def combine_body(r_ref, p_ref, m_ref):
-    l, rows = r_ref.shape[0], r_ref.shape[1]
-    x = jnp.concatenate([r_ref[i] for i in range(l)], axis=0)
-    p = jnp.concatenate([p_ref[i] for i in range(l)], axis=0)
-    y = dot(p, x, 0, 0).astype(BF)
-    g = m_ref.shape[1]
+    message = to_message()
+    for p in range(w_ref.shape[0]):
+        rows = out[2 * p * HELD : 2 * (p + 1) * HELD] * w_ref[p]
+        rows = dot(message, rows.astype(BF)).astype(BF)
+        m_ref[2 * p] = rows[:ROWS]
+        m_ref[2 * p + 1] = rows[ROWS:]
+
+
+def stacked(ref):
+    return jnp.concatenate([ref[i] for i in range(ref.shape[0])], axis=0)
+
+
+def combine_body(r_ref, p_ref, t_ref, m_ref):
+    y = dot(stacked(p_ref), stacked(r_ref), 0, 0).astype(BF)
+    message = jnp.concatenate([y, t_ref[...]], axis=0)
     for i in range(m_ref.shape[0]):
-        m_ref[i] = y[i * g : (i + 1) * g]
-
-
-def resid_body(r_ref, t_ref, o_ref, m_ref):
-    total = r_ref[0].astype(F4)
-    for i in range(1, r_ref.shape[0]):
-        total = total + r_ref[i].astype(F4)
-    layer = total.astype(BF)
-    o_ref[...] = layer
-    resid = (layer.astype(F4) - t_ref[...].astype(F4)).astype(BF)
-    for i in range(m_ref.shape[0]):
-        m_ref[i] = resid
-
-
-def redispatch_body(r_ref, p_ref, m_ref):
-    x = jnp.concatenate([r_ref[i] for i in range(r_ref.shape[0])], axis=0)
+        m_ref[i] = message
+
+
+def resid_body(base_ref, r_ref, p_ref, o_ref, m_ref, layer_ref):
+    l, g = r_ref.shape[0], o_ref.shape[0]
+    total = r_ref[0, : l * g].astype(F4)
+    for i in range(1, l):
+        total = total + r_ref[i, : l * g].astype(F4)
+    layer = total.astype(BF).astype(F4)
+    layer_ref[...] = layer
+    o_ref[...] = layer_ref[pl.ds(pl.multiple_of(base_ref[0] * g, g), g)].astype(BF)
+    target = jnp.concatenate([r_ref[i, l * g :] for i in range(l)], axis=0)
+    resid = (layer - target.astype(F4)).astype(BF)
     for e in range(p_ref.shape[0]):
-        m_ref[e] = dot(p_ref[e], x).astype(BF)
+        m_ref[e] = dot(p_ref[e], resid).astype(BF)
 
 
 def delta_in_body(r_ref, w_ref, out_ref, wd_ref, h_ref, f_ref, g_ref):
-    l, h = w_ref.shape[0], w_ref.shape[1]
+    pairs = w_ref.shape[0]
     n, fs = f_ref.shape[0], f_ref.shape[1] // 4
     slots = h_ref.shape[1]
+    run = 2 * HELD
     rows, tiles = [], []
-    for e in range(l):
-        resid = r_ref[e].astype(F4)[: CAP * h]
-        out = out_ref[e * CAP * h : (e + 1) * CAP * h]
-        column = jnp.sum(resid * out, axis=1, keepdims=True)
-        tiles.append(split3(column_tile(column, h), 8))
-        rows.append(scale_rows(resid, w_ref[e], h))
-    rows.append(jnp.zeros((slots - l * CAP * h, LANES), F4))
+    take, tile = to_slots(), scalars_to_tile()
+    for p in range(pairs):
+        resid = dot(take, pair(r_ref, p))
+        column = jnp.sum(resid * out_ref[p * run : (p + 1) * run], axis=1, keepdims=True)
+        tiles.append(dot(tile, spread(column, HELD)))
+        rows.append(resid * w_ref[p])
+    rows.append(jnp.zeros((slots - pairs * run, LANES), F4))
     scaled = jnp.concatenate(rows, axis=0).astype(BF)
-    half = l // 2
+    half = pairs // 2
     packed = roll(jnp.concatenate(tiles[:half], axis=0), 64) + roll(
         jnp.concatenate(tiles[half:], axis=0), 88
     )
@@ -288,7 +316,7 @@
     dup = (dh * gate * s).astype(BF)
     dgu = jnp.concatenate([dgate, dup], axis=0)
     dgu_ref[...] = dgu
-    held = CAP * h * l
+    held = 2 * HELD * l
     for i in range(n // 2):
         back = dot(dgu, wgu_ref[:, 2 * i * LANES : 2 * (i + 1) * LANES], 0, 0)
         back = back[:held].astype(BF)
@@ -298,17 +326,23 @@
             f_ref[d, fs:] = back[:, own : own + LANES]
 
 
-def back_body(r_ref, dot_ref, m_ref, gd_ref):
-    l, h = dot_ref.shape[0], dot_ref.shape[1]
-    fs = r_ref.shape[1] - CAP * h * l
-    for e in range(l):
-        part = pl.ds(fs + e * CAP * h, CAP * h)
+def back_body(r_ref, dot_ref, m_ref, gd_ref, tick_ref):
+    pairs = dot_ref.shape[0]
+    run = 2 * HELD
+    fs = r_ref.shape[1] - run * pairs
+    message, scalars = to_message(), tile_to_message()
+    for p in range(pairs):
+        part = pl.ds(fs + p * run, run)
         rows = r_ref[0, part].astype(F4)
         for i in range(1, r_ref.shape[0]):
             rows = rows + r_ref[i, part].astype(F4)
-        m_ref[e] = jnp.concatenate([rows, split3(dot_ref[e], 8)], axis=0).astype(BF)
+        rows = dot(message, rows.astype(BF)) + dot(scalars, split3(dot_ref[p], 8).astype(BF))
+        rows = rows.astype(BF)
+        m_ref[2 * p] = rows[:ROWS]
+        m_ref[2 * p + 1] = rows[ROWS:]
     for i in range(r_ref.shape[0]):
         gd_ref[:, i * LANES : (i + 1) * LANES] = r_ref[i, :fs].astype(F4)
+    tick_ref[...] = dot_ref[0]
 
 
 def grads_body(tick_ref, x_ref, dgu_ref, gg_ref, gu_ref):
@@ -323,31 +357,22 @@
         gu_ref[:, part] = grad[fs:]
 
 
-def combine_back_body(base_ref, r_ref, p_ref, ids_ref, m_ref, tick_ref):
-    l, hosts = r_ref.shape[0], m_ref.shape[0]
-    h = hosts
-    g = 32
-    per = LANES // g
-    x = jnp.concatenate([r_ref[i] for i in range(l)], axis=0)
-    p = jnp.concatenate([p_ref[i] for i in range(l)], axis=0)
-    y = dot(p, x, 0, 0)
+def combine_back_body(base_ref, r_ref, p_ref, ids_ref, m_ref):
+    h, l = r_ref.shape[0], m_ref.shape[0]
+    g = LANES // l
+    y = dot(stacked(p_ref), stacked(r_ref), 0, 0)
     ids = ids_ref[...]
-    tick_ref[...] = ids[:, :LANES]
+    i, j = index((ROWS, ROWS))
+    up = onehot(j == HELD + i % NEAR)
     routes = jnp.zeros(ids.shape, F4)
-    for e in range(l):
-        tile = join3(r_ref[e].astype(F4)[CAP * h :], 8)
-        place = p_ref[e].astype(F4)
-        acc = jnp.zeros((h, ids.shape[1]), F4)
-        for c in range(CAP):
-            acc = acc + place[c * h : (c + 1) * h] * tile[:, c : c + 1]
-        at_token = jnp.sum(acc, axis=0, keepdims=True)
-        mine = (base_ref[0] + e).astype(F4)
+    for e in range(h):
+        column = gathered_column(dot(up, r_ref[e]), ROWS)
+        at_token = jnp.sum(p_ref[e].astype(F4) * column, axis=0, keepdims=True)
+        mine = (base_ref[0] + e * l).astype(F4)
         routes = routes + jnp.where(ids == mine, at_token, 0.0)
     at = lane((8, LANES))
-    for i in range(hosts):
-        q = i // per
-        own = roll(routes[:, q * LANES : (q + 1) * LANES], -(i % per) * g)
-        own = split3(jnp.where(at < g, own, 0.0), g)
+    for i in range(l):
+        own = split3(jnp.where(at < g, roll(routes, -i * g), 0.0), g)
         m_ref[i] = jnp.concatenate(
             [y[i * g : (i + 1) * g], own, jnp.zeros((8, LANES), F4)], axis=0
         ).astype(BF)
@@ -372,14 +397,15 @@
     fs, d = w_gate.shape[1], w_gate.shape[2]
     df = tokens.shape[1]
     mean_load = k * g // (h * l)
-    assert df == LANES and g == 32 and k == 8 and h % 8 == 0
+    assert df == LANES and g * l == LANES and k == 8 and l == NEAR
     assert min(g, mean_load + mean_load // 2 + 1) == CAP
     wg, wu, wd = w_gate[0], w_up[0], w_down[0]
     held, slots = CAP * h * l, 8 * h * l
-    base = (lax.axis_index("eh") * l).astype(jnp.int32).reshape(1)
+    pairs = h // 2
+    base = lax.axis_index("el").astype(jnp.int32).reshape(1)
 
     (message,) = call(
-        first_body, [((h, g + 16, df), BF)],
+        first_body, [((l, g + 16, df), BF)],
         base, expert_ids.T, route_weights.T, tokens, smem=(0,), hbm=(1, 2, 3),
         scratch=(
             pltpu.VMEM((k, g), jnp.int32), pltpu.VMEM((k, g), F4), pltpu.VMEM((g, df), BF),
@@ -387,19 +413,19 @@
         ),
         vmem_mib=60, name="first",
     )
-    got = exchange(message, "eh")
+    got = exchange(message, "el")
     wgu, wd = call(
         weights_body, [((2 * fs, d), BF), ((fs, d), BF)], wg, wu, wd, name="weights"
     )
+    to_far = ((h, ROWS, df), BF)
     message, place, ids = call(
-        dispatch_body,
-        [((l, 8 * h, df), BF), ((l, 8 * h, h * g), BF), ((8, h * g), F4)],
+        dispatch_body, [to_far, to_far, ((8, LANES), F4)],
         base, got, smem=(0,), name="dispatch",
     )
-    got = exchange(message, "el")
-    message, w_tile = call(
+    got = exchange(message, "eh")
+    message, scale = call(
         expert_in_body,
-        [((n, fs + held, df), BF), ((l, h, LANES), F4)],
+        [((n, fs + held, df), BF), ((pairs, 2 * HELD, LANES), F4)],
         got, wd, name="expert_in",
     )
     rows = exchange(message, "fsdp")
@@ -412,45 +438,43 @@
     got = exchange(message, "fsdp")
     out, hidden, message = call(
         expert_out_body,
-        [((slots, df), F4), ((n * fs, slots), BF), ((l, 8 * h, df), BF)],
-        got, wd_f, w_tile, name="expert_out",
-    )
-    got = exchange(message, "el")
-    (message,) = call(combine_body, [((h, g, df), BF)], got, place, name="combine")
-    got = exchange(message, "eh")
-    layer_out, message = call(
-        resid_body, [((g, df), BF), ((h, g, df), BF)], got, target, name="resid"
+        [((slots, df), F4), ((n * fs, slots), BF), to_far],
+        got, wd_f, scale, name="expert_out",
     )
     got = exchange(message, "eh")
     (message,) = call(
-        redispatch_body, [((l, 8 * h, df), BF)], got, place, name="redispatch"
+        combine_body, [((l, l * g + g, df), BF)], got, place, target, name="combine"
     )
     got = exchange(message, "el")
+    layer_out, message = call(
+        resid_body, [((g, df), BF), to_far], base, got, place, smem=(0,),
+        scratch=(pltpu.VMEM((l * g, df), F4),), name="resid",
+    )
+    got = exchange(message, "eh")
     message, down = call(
         delta_in_body,
         [(packed, BF), ((n, fs, df), BF)],
-        got, w_tile, out, wd_f, hidden, name="delta_in",
+        got, scale, out, wd_f, hidden, name="delta_in",
     )
     got = exchange(message, "fsdp")
     message, dgu, dots = call(
         delta_body,
-        [((n, fs + held, df), BF), ((2 * fs, slots), BF), ((l, h, LANES), F4)],
+        [((n, fs + held, df), BF), ((2 * fs, slots), BF), ((pairs, 2 * l, LANES), F4)],
         got, gate, up, wgu, down, name="delta",
     )
     got = exchange(message, "fsdp")
-    message, grad_down = call(
-        back_body, [((l, 8 * h, df), BF), ((fs, d), F4)], got, dots, name="back"
-    )
-    got = exchange(message, "el")
-    message, tick = call(
-        combine_back_body,
-        [((h, g + 16, df), BF), ((8, LANES), F4)],
-        base, got, place, ids, smem=(0,), name="combine_back",
+    message, grad_down, tick = call(
+        back_body, [to_far, ((fs, d), F4), ((2 * l, LANES), F4)], got, dots, name="back"
     )
     got = exchange(message, "eh")
     grad_gate, grad_up = call(
         grads_body, [((fs, d), F4)] * 2, tick, rows, dgu, name="grads"
     )
+    (message,) = call(
+        combine_back_body, [((l, g + 16, df), BF)],
+        base, got, place, ids, smem=(0,), name="combine_back",
+    )
+    got = exchange(message, "el")
     grad_tokens, grad_route = call(
         finish_body, [((g, df), BF), ((8, g), F4)], got, name="finish"
     )
@@ -461,7 +485,7 @@
 
 def solution(mesh):
     experts, fsdp = mesh.devices.shape
-    split = Mesh(mesh.devices.reshape(HI, experts // HI, fsdp), ("eh", "el", "fsdp"))
+    split = Mesh(mesh.devices.reshape(experts // NEAR, NEAR, fsdp), ("eh", "el", "fsdp"))
     e = ("eh", "el")
     return jax.shard_map(
         shards,

time: 287 us -> 286 us (level); the launches traced: 282 us -> 285 us
  starting transfers between devices: 12.9 us -> 26.6 us
  blocking collectives: 230 us -> 221 us
    all_to_all x2, starting transfers between devices: 12.9 us -> 26.6 us  [exchange(): return lax.all_to_all(x, axis, split_axis=0, concat_axis=0, tiled=True)]
    all_to_all x10 -> x9, blocking collectives: 230 us -> 221 us  [exchange(): return lax.all_to_all(x, axis, split_axis=0, concat_axis=0, tiled=True)]
    pallas_call x15 -> x14, Pallas kernels: 11.4 us -> 12.1 us  [call(): pl.pallas_call(body, out_shape=shapes, in_specs=specs, out_specs=[pl.Bloc...]
where the time goes in v3:
time: 286 us; the launch traced here: 285 us
  blocking collectives  221 us (77%)
  starting transfers between devices  26.6 us (9%)
  waiting for transfers between devices  21.3 us (7%)
  Pallas kernels  12.1 us (4%)
    all_to_all x9, blocking collectives, exchange(): return lax.all_to_all(x, axis, split_axis=0, concat_axis=0, tiled=True)  221 us
    all_to_all x2, starting transfers between devices, exchange(): return lax.all_to_all(x, axis, split_axis=0, concat_axis=0, tiled=True)  26.6 us
    all_to_all x2, waiting for transfers between devices, exchange(): return lax.all_to_all(x, axis, split_axis=0, concat_axis=0, tiled=True)  21.3 us
    pallas_call x14, Pallas kernels, call(): pl.pallas_call(body, out_shape=shapes, in_specs=specs, out_specs=[pl.Bloc...  12.1 us
  transfers between devices with their start and end apart: 2, of which 2 were waited for; matrix products, arithmetic and copies ran while one was open for 0% of the time, Pallas kernels for 0%

profile of v3, /device:TPU:1, one launch (start us, length us, event | category | flops | bytes accessed | tf_op | source)
XLA Modules:
  0.0 284.8 jit_solution(11407488869621759833)
XLA Ops:
  0.6 1.5 first.1
  2.2 20.6 %all_to_all.55.r_ref = bf16[4,48,128]{2,1,0:T(8,128)(2,1)S(1)} all-to-all(bf16[4,48,128]{2,1,0:T(8,128)(2,1)} %first.1), channel_id=1, replica_groups=mesh['eh'=16,'el'=4,'fsdp'=16] {'el'}, dimensions={0} | all-to-all | bytes 98304 | tf_op jit(solution)/shard_map/all_to_all | solution.py:391
  22.8 1.5 dispatch.1
  24.3 15.5 %all-to-all-start.1 = ((bf16[16,32,128]{2,1,0:T(8,128)(2,1)}), bf16[16,32,128]{2,1,0:T(8,128)(2,1)S(1)}, u32[]{:S(2)}, u32[]{:S(2)}) async-start(bf16[16,32,128]{2,1,0:T(8,128)(2,1)} %get-tuple-element.34), calls=%async_computation.1 | async-start | bytes 262144 | tf_op jit(solution)/shard_map/all_to_all | solution.py:391
  39.8 0.0 copy-start
  39.8 0.9 copy-done
  40.7 0.0 copy-start.1
  40.7 0.9 copy-done.1
  41.6 0.0 copy-start.2
  41.6 0.9 copy-done.2
  42.6 19.4 %all-to-all-done.1.r_ref = bf16[16,32,128]{2,1,0:T(8,128)(2,1)S(1)} async-done(((bf16[16,32,128]{2,1,0:T(8,128)(2,1)}), bf16[16,32,128]{2,1,0:T(8,128)(2,1)S(1)}, u32[]{:S(2)}, u32[]{:S(2)}) %all-to-all-start.1) | async-done | bytes 131104 | tf_op jit(solution)/shard_map/all_to_all | solution.py:391
  62.0 0.3 expert_in.1
  62.4 27.7 %all_to_all.56.r_ref.x_ref = bf16[16,496,128]{2,1,0:T(8,128)(2,1)S(1)} all-to-all(bf16[16,496,128]{2,1,0:T(8,128)(2,1)S(1)} %get-tuple-element.36), channel_id=1, replica_groups=mesh['eh'=16,'el'=4,'fsdp'=16] {'fsdp'}, dimensions={0} | all-to-all | bytes 4063232 | tf_op jit(solution)/shard_map/all_to_all | solution.py:391
  90.1 0.7 hidden.1
  90.8 0.0 copy-start.3
  90.8 13.3 %all_to_all.57.r_ref = bf16[16,192,128]{2,1,0:T(8,128)(2,1)S(1)} all-to-all(bf16[16,192,128]{2,1,0:T(8,128)(2,1)S(1)} %get-tuple-element.38), channel_id=1, replica_groups=mesh['eh'=16,'el'=4,'fsdp'=16] {'fsdp'}, dimensions={0} | all-to-all | bytes 1572864 | tf_op jit(solution)/shard_map/all_to_all | solution.py:391
  104.1 0.5 expert_out.1
  104.7 40.1 %all_to_all.58.r_ref = bf16[16,32,128]{2,1,0:T(8,128)(2,1)S(1)} all-to-all(bf16[16,32,128]{2,1,0:T(8,128)(2,1)S(1)} %get-tuple-element.41), channel_id=1, replica_groups=mesh['eh'=16,'el'=4,'fsdp'=16] {'eh'}, dimensions={0} | all-to-all | bytes 262144 | tf_op jit(solution)/shard_map/all_to_all | solution.py:391
  144.8 0.0 copy-done.3
  144.8 0.2 combine.1
  145.0 14.2 %all_to_all.59.r_ref = bf16[4,160,128]{2,1,0:T(8,128)(2,1)S(1)} all-to-all(bf16[4,160,128]{2,1,0:T(8,128)(2,1)S(1)} %combine.1), channel_id=1, replica_groups=mesh['eh'=16,'el'=4,'fsdp'=16] {'el'}, dimensions={0} | all-to-all | bytes 327680 | tf_op jit(solution)/shard_map/all_to_all | solution.py:391
  159.2 0.7 resid.1
  159.9 26.7 %all_to_all.60.r_ref = bf16[16,32,128]{2,1,0:T(8,128)(2,1)S(1)} all-to-all(bf16[16,32,128]{2,1,0:T(8,128)(2,1)S(1)} %get-tuple-element.44), channel_id=1, replica_groups=mesh['eh'=16,'el'=4,'fsdp'=16] {'eh'}, dimensions={0} | all-to-all | bytes 262144 | tf_op jit(solution)/shard_map/all_to_all | solution.py:391
  186.7 1.6 delta_in.1
  188.3 13.9 %all_to_all.61.r_ref = bf16[16,192,128]{2,1,0:T(8,128)(2,1)S(1)} all-to-all(bf16[16,192,128]{2,1,0:T(8,128)(2,1)S(1)} %get-tuple-element.47), channel_id=1, replica_groups=mesh['eh'=16,'el'=4,'fsdp'=16] {'fsdp'}, dimensions={0} | all-to-all | bytes 1572864 | tf_op jit(solution)/shard_map/all_to_all | solution.py:391
  202.1 0.8 delta.1
  202.9 24.7 %all_to_all.62.r_ref = bf16[16,496,128]{2,1,0:T(8,128)(2,1)S(1)} all-to-all(bf16[16,496,128]{2,1,0:T(8,128)(2,1)S(1)} %get-tuple-element.51), channel_id=1, replica_groups=mesh['eh'=16,'el'=4,'fsdp'=16] {'fsdp'}, dimensions={0} | all-to-all | bytes 4063232 | tf_op jit(solution)/shard_map/all_to_all | solution.py:391
  227.6 1.1 back.1
  228.7 40.0 %all_to_all.63.r_ref = bf16[16,32,128]{2,1,0:T(8,128)(2,1)S(1)} all-to-all(bf16[16,32,128]{2,1,0:T(8,128)(2,1)S(1)} %get-tuple-element.53), channel_id=1, replica_groups=mesh['eh'=16,'el'=4,'fsdp'=16] {'eh'}, dimensions={0} | all-to-all | bytes 262144 | tf_op jit(solution)/shard_map/all_to_all | solution.py:391
  268.7 1.2 combine_back.1
  269.8 11.1 %all-to-all-start.10 = ((bf16[4,48,128]{2,1,0:T(8,128)(2,1)}), bf16[4,48,128]{2,1,0:T(8,128)(2,1)S(1)}, u32[]{:S(2)}, u32[]{:S(2)}) async-start(bf16[4,48,128]{2,1,0:T(8,128)(2,1)} %combine_back.1), calls=%async_computation.10 | async-start | bytes 98304 | tf_op jit(solution)/shard_map/all_to_all | solution.py:391
  280.9 1.3 grads.1
  282.2 1.9 all-to-all-done.10.r_ref
  284.1 0.7 finish.1
  (1 shorter events, 0.0 us)
Async XLA Ops:
  24.3 37.8 %all-to-all-start.1 = ((bf16[16,32,128]{2,1,0:T(8,128)(2,1)}), bf16[16,32,128]{2,1,0:T(8,128)(2,1)S(1)}, u32[]{:S(2)}, u32[]{:S(2)}) async-start(bf16[16,32,128]{2,1,0:T(8,128)(2,1)} %get-tuple-element.34), calls=%async_computation.1 | async-start | bytes 262144 | tf_op jit(solution)/shard_map/all_to_all | solution.py:391
  39.8 0.9 copy-start
  40.7 0.9 copy-start.1
  41.6 0.9 copy-start.2
  90.8 54.0 %copy-start.3 = (bf16[32,128]{1,0:T(8,128)(2,1)S(1)}, bf16[32,128]{1,0:T(8,128)(2,1)}, u32[]{:S(2)}) copy-start(bf16[32,128]{1,0:T(8,128)(2,1)} %t_ref.1) | copy-start | bytes 24580
  269.8 14.3 %all-to-all-start.10 = ((bf16[4,48,128]{2,1,0:T(8,128)(2,1)}), bf16[4,48,128]{2,1,0:T(8,128)(2,1)S(1)}, u32[]{:S(2)}, u32[]{:S(2)}) async-start(bf16[4,48,128]{2,1,0:T(8,128)(2,1)} %combine_back.1), calls=%async_computation.10 | async-start | bytes 98304 | tf_op jit(solution)/shard_map/all_to_all | solution.py:391

commit v4 on v2

--- a/solution.py
+++ b/solution.py
@@ -106,8 +106,7 @@
     for i, part in enumerate((ids_ref[...].astype(F4).astype(BF), hi, mid, low)):
         move = jnp.where(col == row + i * g, 1.0, 0.0).astype(BF)
         meta = meta + dot(part, move)
-    tail = jnp.concatenate([meta, jnp.zeros_like(meta)], axis=0).astype(BF)
-    message = jnp.concatenate([t_ref[...], tail], axis=0)
+    message = jnp.concatenate([t_ref[...].astype(F4), meta], axis=0).astype(BF)
     for i in range(m_ref.shape[0]):
         m_ref[i] = message
 
@@ -195,17 +194,28 @@
     gate, up = total[:fs], total[fs:]
     gate_ref[...] = gate
     up_ref[...] = up
-    hidden = (gate * jax.nn.sigmoid(gate) * up).astype(BF)
-    message = blocks_to_rows(hidden)
+    hidden = gate * jax.nn.sigmoid(gate) * up
+    last = hidden[:, 3 * LANES :]
+    last = last[: fs // 2] + roll(last[fs // 2 :], LANES // 2)
+    message = blocks_to_rows(hidden[:, : 3 * LANES])
+    message = jnp.concatenate([message, last], axis=0).astype(BF)
     for d in range(n):
         f_ref[d] = message
         wd_ref[d * fs : (d + 1) * fs] = r_ref[d, :fs]
 
 
 def expert_out_body(r_ref, wd_ref, w_ref, out_ref, h_ref, m_ref):
-    n, fs = r_ref.shape[0], r_ref.shape[1] // 4
-    l, h = w_ref.shape[0], w_ref.shape[1]
-    hidden = jnp.concatenate([rows_to_blocks(r_ref[i], fs) for i in range(n)], axis=0)
+    n, l, h = r_ref.shape[0], w_ref.shape[0], w_ref.shape[1]
+    fs = wd_ref.shape[0] // n
+    parts = []
+    for i in range(n):
+        v = r_ref[i].astype(F4)
+        last = v[3 * fs :]
+        left = lane(last.shape) < LANES // 2
+        halves = [jnp.where(left, x, 0.0) for x in (last, roll(last, LANES // 2))]
+        v = jnp.concatenate([v[: 3 * fs]] + halves, axis=0)
+        parts.append(rows_to_blocks(v, fs).astype(BF))
+    hidden = jnp.concatenate(parts, axis=0)
     h_ref[...] = hidden
     out = dot(hidden, wd_ref[...], 0, 0)
     out_ref[...] = out
@@ -301,11 +311,11 @@
 def back_body(r_ref, dot_ref, m_ref, gd_ref):
     l, h = dot_ref.shape[0], dot_ref.shape[1]
     fs = r_ref.shape[1] - CAP * h * l
-    for e in range(l):
-        part = pl.ds(fs + e * CAP * h, CAP * h)
-        rows = r_ref[0, part].astype(F4)
-        for i in range(1, r_ref.shape[0]):
-            rows = rows + r_ref[i, part].astype(F4)
+    total = r_ref[0, fs:].astype(F4)
+    for i in range(1, r_ref.shape[0]):
+        total = total + r_ref[i, fs:].astype(F4)
+    for e in range(l):
+        rows = total[e * CAP * h : (e + 1) * CAP * h]
         m_ref[e] = jnp.concatenate([rows, split3(dot_ref[e], 8)], axis=0).astype(BF)
     for i in range(r_ref.shape[0]):
         gd_ref[:, i * LANES : (i + 1) * LANES] = r_ref[i, :fs].astype(F4)
@@ -348,9 +358,7 @@
         q = i // per
         own = roll(routes[:, q * LANES : (q + 1) * LANES], -(i % per) * g)
         own = split3(jnp.where(at < g, own, 0.0), g)
-        m_ref[i] = jnp.concatenate(
-            [y[i * g : (i + 1) * g], own, jnp.zeros((8, LANES), F4)], axis=0
-        ).astype(BF)
+        m_ref[i] = jnp.concatenate([y[i * g : (i + 1) * g], own], axis=0).astype(BF)
 
 
 def finish_body(r_ref, t_ref, g_ref):
@@ -379,7 +387,7 @@
     base = (lax.axis_index("eh") * l).astype(jnp.int32).reshape(1)
 
     (message,) = call(
-        first_body, [((h, g + 16, df), BF)],
+        first_body, [((h, g + 8, df), BF)],
         base, expert_ids.T, route_weights.T, tokens, smem=(0,), hbm=(1, 2, 3),
         scratch=(
             pltpu.VMEM((k, g), jnp.int32), pltpu.VMEM((k, g), F4), pltpu.VMEM((g, df), BF),
@@ -404,9 +412,10 @@
     )
     rows = exchange(message, "fsdp")
     packed = (n, fs * slots // LANES, LANES)
+    half_packed = (n, fs * slots // LANES - fs // 2, LANES)
     gate, up, wd_f, message = call(
         hidden_body,
-        [((fs, slots), F4), ((fs, slots), F4), ((n * fs, df), BF), (packed, BF)],
+        [((fs, slots), F4), ((fs, slots), F4), ((n * fs, df), BF), (half_packed, BF)],
         rows, wgu, name="hidden",
     )
     got = exchange(message, "fsdp")
@@ -444,7 +453,7 @@
     got = exchange(message, "el")
     message, tick = call(
         combine_back_body,
-        [((h, g + 16, df), BF), ((8, LANES), F4)],
+        [((h, g + 8, df), BF), ((8, LANES), F4)],
         base, got, place, ids, smem=(0,), name="combine_back",
     )
     got = exchange(message, "eh")

time: 287 us -> 284 us (0.990)
  no operation moved by 1% of the time
where the time goes in v4:
time: 284 us; the launch traced here: 280 us
  blocking collectives  229 us (81%)
  waiting for transfers between devices  23.8 us (8%)
  starting transfers between devices  11.9 us (4%)
  Pallas kernels  11.6 us (4%)
    all_to_all x10, blocking collectives, exchange(): return lax.all_to_all(x, axis, split_axis=0, concat_axis=0, tiled=True)  229 us
    all_to_all x2, waiting for transfers between devices, exchange(): return lax.all_to_all(x, axis, split_axis=0, concat_axis=0, tiled=True)  23.8 us
    all_to_all x2, starting transfers between devices, exchange(): return lax.all_to_all(x, axis, split_axis=0, concat_axis=0, tiled=True)  11.9 us
    pallas_call x15, Pallas kernels, call(): pl.pallas_call(body, out_shape=shapes, in_specs=specs, out_specs=[pl.Bloc...  11.6 us
  transfers between devices with their start and end apart: 2, of which 2 were waited for; matrix products, arithmetic and copies ran while one was open for 0% of the time, Pallas kernels for 0%

profile of v4, /device:TPU:1, one launch (start us, length us, event | category | flops | bytes accessed | tf_op | source)
XLA Modules:
  0.0 280.2 jit_solution(5927183032035668543)
XLA Ops:
  0.6 1.5 first.1
  2.2 51.2 %all_to_all.60.r_ref = bf16[8,40,128]{2,1,0:T(8,128)(2,1)S(1)} all-to-all(bf16[8,40,128]{2,1,0:T(8,128)(2,1)} %first.1), channel_id=1, replica_groups=mesh['eh'=8,'el'=8,'fsdp'=16] {'eh'}, dimensions={0} | all-to-all | bytes 163840 | tf_op jit(solution)/shard_map/all_to_all | solution.py:374
  53.4 1.1 dispatch.1
  54.5 8.5 %all-to-all-start.1 = ((bf16[8,64,128]{2,1,0:T(8,128)(2,1)}), bf16[8,64,128]{2,1,0:T(8,128)(2,1)S(1)}, u32[]{:S(2)}, u32[]{:S(2)}) async-start(bf16[8,64,128]{2,1,0:T(8,128)(2,1)} %get-tuple-element.35), calls=%async_computation.1 | async-start | bytes 262144 | tf_op jit(solution)/shard_map/all_to_all | solution.py:374
  63.0 0.0 copy-start
  63.0 0.9 copy-done
  63.9 0.0 copy-start.1
  63.9 0.9 copy-done.1
  64.8 0.0 copy-start.2
  64.8 0.9 copy-done.2
  65.8 3.0 %all-to-all-done.1.r_ref = bf16[8,64,128]{2,1,0:T(8,128)(2,1)S(1)} async-done(((bf16[8,64,128]{2,1,0:T(8,128)(2,1)}), bf16[8,64,128]{2,1,0:T(8,128)(2,1)S(1)}, u32[]{:S(2)}, u32[]{:S(2)}) %all-to-all-start.1) | async-done | bytes 131104 | tf_op jit(solution)/shard_map/all_to_all | solution.py:374
  68.8 0.3 expert_in.1
  69.1 32.1 %all_to_all.61.r_ref.x_ref = bf16[16,496,128]{2,1,0:T(8,128)(2,1)S(1)} all-to-all(bf16[16,496,128]{2,1,0:T(8,128)(2,1)S(1)} %get-tuple-element.37), channel_id=1, replica_groups=mesh['eh'=8,'el'=8,'fsdp'=16] {'fsdp'}, dimensions={0} | all-to-all | bytes 4063232 | tf_op jit(solution)/shard_map/all_to_all | solution.py:374
  101.2 0.7 hidden.1
  101.9 0.0 copy-start.3
  101.9 14.9 %all_to_all.62.r_ref = bf16[16,168,128]{2,1,0:T(8,128)(2,1)S(1)} all-to-all(bf16[16,168,128]{2,1,0:T(8,128)(2,1)S(1)} %get-tuple-element.39), channel_id=1, replica_groups=mesh['eh'=8,'el'=8,'fsdp'=16] {'fsdp'}, dimensions={0} | all-to-all | bytes 1376256 | tf_op jit(solution)/shard_map/all_to_all | solution.py:374
  116.8 0.5 expert_out.1
  117.3 11.7 %all_to_all.63.r_ref = bf16[8,64,128]{2,1,0:T(8,128)(2,1)S(1)} all-to-all(bf16[8,64,128]{2,1,0:T(8,128)(2,1)S(1)} %get-tuple-element.42), channel_id=1, replica_groups=mesh['eh'=8,'el'=8,'fsdp'=16] {'el'}, dimensions={0} | all-to-all | bytes 262144 | tf_op jit(solution)/shard_map/all_to_all | solution.py:374
  129.0 0.3 combine.1
  129.2 24.4 %all_to_all.64.r_ref = bf16[8,32,128]{2,1,0:T(8,128)(2,1)S(1)} all-to-all(bf16[8,32,128]{2,1,0:T(8,128)(2,1)S(1)} %combine.1), channel_id=1, replica_groups=mesh['eh'=8,'el'=8,'fsdp'=16] {'eh'}, dimensions={0} | all-to-all | bytes 131072 | tf_op jit(solution)/shard_map/all_to_all | solution.py:374
  153.7 0.0 copy-done.3
  153.7 0.6 resid.1
  154.3 25.8 %all_to_all.65.r_ref = bf16[8,32,128]{2,1,0:T(8,128)(2,1)S(1)} all-to-all(bf16[8,32,128]{2,1,0:T(8,128)(2,1)S(1)} %get-tuple-element.45), channel_id=1, replica_groups=mesh['eh'=8,'el'=8,'fsdp'=16] {'eh'}, dimensions={0} | all-to-all | bytes 131072 | tf_op jit(solution)/shard_map/all_to_all | solution.py:374
  180.1 0.2 redispatch.1
  180.3 13.3 %all_to_all.66.r_ref = bf16[8,64,128]{2,1,0:T(8,128)(2,1)S(1)} all-to-all(bf16[8,64,128]{2,1,0:T(8,128)(2,1)S(1)} %redispatch.1), channel_id=1, replica_groups=mesh['eh'=8,'el'=8,'fsdp'=16] {'el'}, dimensions={0} | all-to-all | bytes 262144 | tf_op jit(solution)/shard_map/all_to_all | solution.py:374
  193.6 1.3 delta_in.1
  195.0 15.5 %all_to_all.67.r_ref = bf16[16,192,128]{2,1,0:T(8,128)(2,1)S(1)} all-to-all(bf16[16,192,128]{2,1,0:T(8,128)(2,1)S(1)} %get-tuple-element.48), channel_id=1, replica_groups=mesh['eh'=8,'el'=8,'fsdp'=16] {'fsdp'}, dimensions={0} | all-to-all | bytes 1572864 | tf_op jit(solution)/shard_map/all_to_all | solution.py:374
  210.5 0.8 delta.1
  211.3 28.1 %all_to_all.68.r_ref = bf16[16,496,128]{2,1,0:T(8,128)(2,1)S(1)} all-to-all(bf16[16,496,128]{2,1,0:T(8,128)(2,1)S(1)} %get-tuple-element.52), channel_id=1, replica_groups=mesh['eh'=8,'el'=8,'fsdp'=16] {'fsdp'}, dimensions={0} | all-to-all | bytes 4063232 | tf_op jit(solution)/shard_map/all_to_all | solution.py:374
  239.3 1.1 back.1
  240.5 12.5 %all_to_all.69.r_ref = bf16[8,64,128]{2,1,0:T(8,128)(2,1)S(1)} all-to-all(bf16[8,64,128]{2,1,0:T(8,128)(2,1)S(1)} %get-tuple-element.54), channel_id=1, replica_groups=mesh['eh'=8,'el'=8,'fsdp'=16] {'el'}, dimensions={0} | all-to-all | bytes 262144 | tf_op jit(solution)/shard_map/all_to_all | solution.py:374
  252.9 1.1 combine_back.1
  254.0 3.4 %all-to-all-start.11 = ((bf16[8,40,128]{2,1,0:T(8,128)(2,1)}), bf16[8,40,128]{2,1,0:T(8,128)(2,1)S(1)}, u32[]{:S(2)}, u32[]{:S(2)}) async-start(bf16[8,40,128]{2,1,0:T(8,128)(2,1)} %get-tuple-element.56), calls=%async_computation.11 | async-start | bytes 163840 | tf_op jit(solution)/shard_map/all_to_all | solution.py:374
  257.4 1.3 grads.1
  258.7 20.8 %all-to-all-done.11.r_ref = bf16[8,40,128]{2,1,0:T(8,128)(2,1)S(1)} async-done(((bf16[8,40,128]{2,1,0:T(8,128)(2,1)}), bf16[8,40,128]{2,1,0:T(8,128)(2,1)S(1)}, u32[]{:S(2)}, u32[]{:S(2)}) %all-to-all-start.11) | async-done | bytes 81952 | tf_op jit(solution)/shard_map/all_to_all | solution.py:374
  279.5 0.7 finish.1
  (1 shorter events, 0.0 us)
Async XLA Ops:
  54.5 14.3 %all-to-all-start.1 = ((bf16[8,64,128]{2,1,0:T(8,128)(2,1)}), bf16[8,64,128]{2,1,0:T(8,128)(2,1)S(1)}, u32[]{:S(2)}, u32[]{:S(2)}) async-start(bf16[8,64,128]{2,1,0:T(8,128)(2,1)} %get-tuple-element.35), calls=%async_computation.1 | async-start | bytes 262144 | tf_op jit(solution)/shard_map/all_to_all | solution.py:374
  63.0 0.9 copy-start
  63.9 0.9 copy-start.1
  64.8 0.9 copy-start.2
  101.9 51.8 %copy-start.3 = (bf16[32,128]{1,0:T(8,128)(2,1)S(1)}, bf16[32,128]{1,0:T(8,128)(2,1)}, u32[]{:S(2)}) copy-start(bf16[32,128]{1,0:T(8,128)(2,1)} %t_ref.1) | copy-start | bytes 24580
  254.0 25.5 %all-to-all-start.11 = ((bf16[8,40,128]{2,1,0:T(8,128)(2,1)}), bf16[8,40,128]{2,1,0:T(8,128)(2,1)S(1)}, u32[]{:S(2)}, u32[]{:S(2)}) async-start(bf16[8,40,128]{2,1,0:T(8,128)(2,1)} %get-tuple-element.56), calls=%async_computation.11 | async-start | bytes 163840 | tf_op jit(solution)/shard_map/all_to_all | solution.py:374

commit v5 on v4

--- a/solution.py
+++ b/solution.py
@@ -118,7 +118,7 @@
     wd_out_ref[...] = wd_ref[...]
 
 
-def dispatch_body(base_ref, r_ref, m_ref, p_ref, ids_ref):
+def dispatch_body(base_ref, r_ref, m_ref):
     h, l = r_ref.shape[0], m_ref.shape[0]
     g = 32
     width = h * g
@@ -138,8 +138,7 @@
 
     ids = gathered(metas, 0)
     weights = gathered([join3(m, g) for m in metas], g)
-    ids_ref[...] = ids
-    mine = (lax.broadcasted_iota(jnp.int32, (l, width), 0) + base_ref[0]).astype(F4)
+    mine = (lax.broadcasted_iota(jnp.int32, (l, width), 0) * h + base_ref[0]).astype(F4)
     named = jnp.zeros((l, width), F4)
     weight_at = jnp.zeros((l, width), F4)
     for k in range(8):
@@ -153,28 +152,40 @@
     rank = jnp.where(named > 0.0, rank, -1.0)
     block = lane((h, width)) // g == lax.broadcasted_iota(jnp.int32, (h, width), 0)
     x = jnp.concatenate([r_ref[i][:g] for i in range(h)], axis=0)
+    number = (lane((1, width)) % g + 1).astype(F4)
     for e in range(l):
         own = jnp.broadcast_to(rank[e : e + 1], (h, width))
         place = jnp.concatenate(
             [jnp.where(block & (own == float(c)), 1.0, 0.0) for c in range(8)], axis=0
         )
         column = jnp.sum(place * weight_at[e : e + 1], axis=1, keepdims=True)
-        place = place.astype(BF)
-        p_ref[e] = place
-        rows = dot(place, x)
-        tile = split3(column_tile(column, h), 8)
+        token = jnp.sum(place * number, axis=1, keepdims=True)
+        rows = dot(place.astype(BF), x)
+        tile = split3(column_tile(column, h), 8) + roll(column_tile(token, h), 24)
         m_ref[e] = jnp.concatenate([rows[: CAP * h], tile], axis=0).astype(BF)
 
 
-def expert_in_body(r_ref, wd_ref, f_ref, w_ref):
-    l, h = r_ref.shape[0], r_ref.shape[1] // 8
+def expert_in_body(r_ref, wd_ref, f_ref, w_ref, k_ref):
+    h, l = r_ref.shape[0], w_ref.shape[0]
     fs = wd_ref.shape[0]
-    rows = []
-    for e in range(l):
+    run = CAP * l
+    rows, tiles = [], []
+    for e in range(h):
         v = r_ref[e].astype(F4)
-        rows.append(v[: CAP * h])
-        w_ref[e] = join3(v[CAP * h :], 8)
-    x = jnp.concatenate(rows, axis=0).astype(BF)
+        rows.append(v[:run])
+        tiles.append(v[run:])
+    i = lax.broadcasted_iota(jnp.int32, (h * run, LANES), 0)
+    source = (i % h * run + i % run // h * l + i // run)[:, :1]
+    move = jnp.where(lane((h * run, h * run)) == source, 1.0, 0.0).astype(BF)
+    x = dot(move, jnp.concatenate(rows, axis=0).astype(BF)).astype(BF)
+    i = lax.broadcasted_iota(jnp.int32, (h * l, h * l), 0)
+    move = jnp.where(lane((h * l, h * l)) == i % h * l + i // h, 1.0, 0.0).astype(BF)
+    meta = dot(move, jnp.concatenate(tiles, axis=0).astype(BF))
+    weights = join3(meta, 8)
+    tokens = jnp.where(lane(meta.shape) < CAP, roll(meta, -24), 0.0)
+    for e in range(l):
+        w_ref[e] = weights[e * h : (e + 1) * h]
+        k_ref[e] = tokens[e * h : (e + 1) * h]
     for d in range(f_ref.shape[0]):
         f_ref[d, :fs] = wd_ref[:, d * LANES : (d + 1) * LANES]
         f_ref[d, fs:] = x
@@ -204,7 +215,7 @@
         wd_ref[d * fs : (d + 1) * fs] = r_ref[d, :fs]
 
 
-def expert_out_body(r_ref, wd_ref, w_ref, out_ref, h_ref, m_ref):
+def expert_out_body(r_ref, wd_ref, w_ref, k_ref, out_ref, h_ref, m_ref):
     n, l, h = r_ref.shape[0], w_ref.shape[0], w_ref.shape[1]
     fs = wd_ref.shape[0] // n
     parts = []
@@ -222,16 +233,25 @@
     for e in range(l):
         rows = out[e * CAP * h : (e + 1) * CAP * h]
         rows = scale_rows(rows, w_ref[e], h)
-        m_ref[e] = jnp.concatenate([rows, jnp.zeros((h, LANES), F4)], axis=0).astype(BF)
-
-
-def combine_body(r_ref, p_ref, m_ref):
-    l, rows = r_ref.shape[0], r_ref.shape[1]
+        m_ref[e] = jnp.concatenate([rows, k_ref[e]], axis=0).astype(BF)
+
+
+def combine_body(r_ref, m_ref, p_ref):
+    l, h, g = r_ref.shape[0], m_ref.shape[0], m_ref.shape[1]
+    shape = (h, h * g)
+    block = lane(shape) // g == lax.broadcasted_iota(jnp.int32, shape, 0)
+    number = jnp.where(block, lane(shape) % g + 1, 0).astype(F4)
+    number = jnp.where(block, number, -1.0)
+    places = []
+    for e in range(l):
+        tile = r_ref[e].astype(F4)[CAP * h :]
+        place = [jnp.where(number == tile[:, c : c + 1], 1.0, 0.0) for c in range(CAP)]
+        place = jnp.concatenate(place + [jnp.zeros(shape, F4)], axis=0).astype(BF)
+        p_ref[e] = place
+        places.append(place)
     x = jnp.concatenate([r_ref[i] for i in range(l)], axis=0)
-    p = jnp.concatenate([p_ref[i] for i in range(l)], axis=0)
-    y = dot(p, x, 0, 0).astype(BF)
-    g = m_ref.shape[1]
-    for i in range(m_ref.shape[0]):
+    y = dot(jnp.concatenate(places, axis=0), x, 0, 0).astype(BF)
+    for i in range(h):
         m_ref[i] = y[i * g : (i + 1) * g]
 
 
@@ -333,41 +353,46 @@
         gu_ref[:, part] = grad[fs:]
 
 
-def combine_back_body(base_ref, r_ref, p_ref, ids_ref, m_ref, tick_ref):
-    l, hosts = r_ref.shape[0], m_ref.shape[0]
-    h = hosts
-    g = 32
+def combine_back_body(r_ref, p_ref, m_ref, tick_ref):
+    l, h = r_ref.shape[0], m_ref.shape[0]
+    g = p_ref.shape[2] // h
     per = LANES // g
     x = jnp.concatenate([r_ref[i] for i in range(l)], axis=0)
     p = jnp.concatenate([p_ref[i] for i in range(l)], axis=0)
     y = dot(p, x, 0, 0)
-    ids = ids_ref[...]
-    tick_ref[...] = ids[:, :LANES]
-    routes = jnp.zeros(ids.shape, F4)
+    shape = (l, h * g)
+    routes = jnp.zeros(shape, F4)
+    row = lax.broadcasted_iota(jnp.int32, shape, 0)
     for e in range(l):
         tile = join3(r_ref[e].astype(F4)[CAP * h :], 8)
         place = p_ref[e].astype(F4)
-        acc = jnp.zeros((h, ids.shape[1]), F4)
+        acc = jnp.zeros((h, h * g), F4)
         for c in range(CAP):
             acc = acc + place[c * h : (c + 1) * h] * tile[:, c : c + 1]
-        at_token = jnp.sum(acc, axis=0, keepdims=True)
-        mine = (base_ref[0] + e).astype(F4)
-        routes = routes + jnp.where(ids == mine, at_token, 0.0)
-    at = lane((8, LANES))
-    for i in range(hosts):
+        routes = jnp.where(row == e, jnp.sum(acc, axis=0, keepdims=True), routes)
+    tick_ref[...] = routes[:, :LANES]
+    at = lane((l, LANES))
+    for i in range(h):
         q = i // per
         own = roll(routes[:, q * LANES : (q + 1) * LANES], -(i % per) * g)
         own = split3(jnp.where(at < g, own, 0.0), g)
         m_ref[i] = jnp.concatenate([y[i * g : (i + 1) * g], own], axis=0).astype(BF)
 
 
-def finish_body(r_ref, t_ref, g_ref):
-    total = r_ref[0].astype(F4)
-    for i in range(1, r_ref.shape[0]):
-        total = total + r_ref[i].astype(F4)
-    rows = t_ref.shape[0]
-    t_ref[...] = total[:rows].astype(BF)
-    g_ref[...] = join3(total[rows : rows + 8], rows)[:, :rows]
+def finish_body(r_ref, ids_ref, t_ref, g_ref):
+    h, rows = r_ref.shape[0], t_ref.shape[0]
+    l = r_ref.shape[1] - rows
+    ids = ids_ref[...]
+    total = jnp.zeros((rows, LANES), F4)
+    routes = jnp.zeros(ids.shape, F4)
+    for i in range(h):
+        v = r_ref[i].astype(F4)
+        total = total + v[:rows]
+        tile = join3(v[rows:], rows)[:, :rows]
+        for e in range(l):
+            routes = routes + jnp.where(ids == i * l + e, tile[e : e + 1], 0.0)
+    t_ref[...] = total.astype(BF)
+    g_ref[...] = routes
 
 
 def exchange(x, axis):
@@ -380,14 +405,14 @@
     fs, d = w_gate.shape[1], w_gate.shape[2]
     df = tokens.shape[1]
     mean_load = k * g // (h * l)
-    assert df == LANES and g == 32 and k == 8 and h % 8 == 0
+    assert df == LANES and g == 32 and k == 8 and h == 8 and l == 8
     assert min(g, mean_load + mean_load // 2 + 1) == CAP
     wg, wu, wd = w_gate[0], w_up[0], w_down[0]
     held, slots = CAP * h * l, 8 * h * l
-    base = (lax.axis_index("eh") * l).astype(jnp.int32).reshape(1)
+    base = lax.axis_index("el").astype(jnp.int32).reshape(1)
 
     (message,) = call(
-        first_body, [((h, g + 8, df), BF)],
+        first_body, [((l, g + 8, df), BF)],
         base, expert_ids.T, route_weights.T, tokens, smem=(0,), hbm=(1, 2, 3),
         scratch=(
             pltpu.VMEM((k, g), jnp.int32), pltpu.VMEM((k, g), F4), pltpu.VMEM((g, df), BF),
@@ -395,19 +420,17 @@
         ),
         vmem_mib=60, name="first",
     )
-    got = exchange(message, "eh")
+    got = exchange(message, "el")
     wgu, wd = call(
         weights_body, [((2 * fs, d), BF), ((fs, d), BF)], wg, wu, wd, name="weights"
     )
-    message, place, ids = call(
-        dispatch_body,
-        [((l, 8 * h, df), BF), ((l, 8 * h, h * g), BF), ((8, h * g), F4)],
-        base, got, smem=(0,), name="dispatch",
-    )
-    got = exchange(message, "el")
-    message, w_tile = call(
+    (message,) = call(
+        dispatch_body, [((h, 8 * l, df), BF)], base, got, smem=(0,), name="dispatch"
+    )
+    got = exchange(message, "eh")
+    message, w_tile, token_tile = call(
         expert_in_body,
-        [((n, fs + held, df), BF), ((l, h, LANES), F4)],
+        [((n, fs + held, df), BF), ((l, h, LANES), F4), ((l, h, LANES), F4)],
         got, wd, name="expert_in",
     )
     rows = exchange(message, "fsdp")
@@ -422,10 +445,12 @@
     out, hidden, message = call(
         expert_out_body,
         [((slots, df), F4), ((n * fs, slots), BF), ((l, 8 * h, df), BF)],
-        got, wd_f, w_tile, name="expert_out",
+        got, wd_f, w_tile, token_tile, name="expert_out",
     )
     got = exchange(message, "el")
-    (message,) = call(combine_body, [((h, g, df), BF)], got, place, name="combine")
+    message, place = call(
+        combine_body, [((h, g, df), BF), ((l, 8 * h, h * g), BF)], got, name="combine"
+    )
     got = exchange(message, "eh")
     layer_out, message = call(
         resid_body, [((g, df), BF), ((h, g, df), BF)], got, target, name="resid"
@@ -454,14 +479,14 @@
     message, tick = call(
         combine_back_body,
         [((h, g + 8, df), BF), ((8, LANES), F4)],
-        base, got, place, ids, smem=(0,), name="combine_back",
+        got, place, name="combine_back",
     )
     got = exchange(message, "eh")
     grad_gate, grad_up = call(
         grads_body, [((fs, d), F4)] * 2, tick, rows, dgu, name="grads"
     )
     grad_tokens, grad_route = call(
-        finish_body, [((g, df), BF), ((8, g), F4)], got, name="finish"
+        finish_body, [((g, df), BF), ((8, g), F4)], got, expert_ids.T, name="finish"
     )
     return (
         layer_out, grad_tokens, grad_route.T, grad_gate[None], grad_up[None], grad_down[None]

time: 284 us -> 287 us (1.011)
  blocking collectives: 229 us -> 207 us
  waiting for transfers between devices: 23.8 us -> 42.4 us
  starting transfers between devices: 11.9 us -> 18.8 us
    all_to_all x10, blocking collectives: 229 us -> 207 us  [exchange(): return lax.all_to_all(x, axis, split_axis=0, concat_axis=0, tiled=True)]
    all_to_all x2, waiting for transfers between devices: 23.8 us -> 42.4 us  [exchange(): return lax.all_to_all(x, axis, split_axis=0, concat_axis=0, tiled=True)]
    all_to_all x2, starting transfers between devices: 11.9 us -> 18.8 us  [exchange(): return lax.all_to_all(x, axis, split_axis=0, concat_axis=0, tiled=True)]
where the time goes in v5:
time: 287 us; the launch traced here: 283 us
  blocking collectives  207 us (72%)
  waiting for transfers between devices  42.4 us (15%)
  starting transfers between devices  18.8 us (7%)
  Pallas kernels  12.1 us (4%)
    all_to_all x10, blocking collectives, exchange(): return lax.all_to_all(x, axis, split_axis=0, concat_axis=0, tiled=True)  207 us
    all_to_all x2, waiting for transfers between devices, exchange(): return lax.all_to_all(x, axis, split_axis=0, concat_axis=0, tiled=True)  42.4 us
    all_to_all x2, starting transfers between devices, exchange(): return lax.all_to_all(x, axis, split_axis=0, concat_axis=0, tiled=True)  18.8 us
    pallas_call x15, Pallas kernels, call(): pl.pallas_call(body, out_shape=shapes, in_specs=specs, out_specs=[pl.Bloc...  12.1 us
  transfers between devices with their start and end apart: 2, of which 2 were waited for; matrix products, arithmetic and copies ran while one was open for 0% of the time, Pallas kernels for 0%

profile of v5, /device:TPU:1, one launch (start us, length us, event | category | flops | bytes accessed | tf_op | source)
XLA Modules:
  0.0 283.4 jit_solution(692260748664747004)
XLA Ops:
  0.6 1.5 first.1
  2.2 22.7 %all_to_all.60.r_ref = bf16[8,40,128]{2,1,0:T(8,128)(2,1)S(1)} all-to-all(bf16[8,40,128]{2,1,0:T(8,128)(2,1)} %first.1), channel_id=1, replica_groups=mesh['eh'=8,'el'=8,'fsdp'=16] {'el'}, dimensions={0} | all-to-all | bytes 163840 | tf_op jit(solution)/shard_map/all_to_all | solution.py:399
  24.8 1.2 dispatch.1
  26.0 15.4 %all-to-all-start.1 = ((bf16[8,64,128]{2,1,0:T(8,128)(2,1)}), bf16[8,64,128]{2,1,0:T(8,128)(2,1)S(1)}, u32[]{:S(2)}, u32[]{:S(2)}) async-start(bf16[8,64,128]{2,1,0:T(8,128)(2,1)} %dispatch.1), calls=%async_computation.1 | async-start | bytes 262144 | tf_op jit(solution)/shard_map/all_to_all | solution.py:399
  41.4 0.0 copy-start
  41.4 0.9 copy-done
  42.3 0.0 copy-start.1
  42.3 0.9 copy-done.1
  43.3 0.0 copy-start.2
  43.3 0.9 copy-done.2
  44.2 21.6 %all-to-all-done.1.r_ref = bf16[8,64,128]{2,1,0:T(8,128)(2,1)S(1)} async-done(((bf16[8,64,128]{2,1,0:T(8,128)(2,1)}), bf16[8,64,128]{2,1,0:T(8,128)(2,1)S(1)}, u32[]{:S(2)}, u32[]{:S(2)}) %all-to-all-start.1) | async-done | bytes 131104 | tf_op jit(solution)/shard_map/all_to_all | solution.py:399
  65.8 0.6 expert_in.1
  66.4 27.8 %all_to_all.61.r_ref.x_ref = bf16[16,496,128]{2,1,0:T(8,128)(2,1)S(1)} all-to-all(bf16[16,496,128]{2,1,0:T(8,128)(2,1)S(1)} %get-tuple-element.36), channel_id=1, replica_groups=mesh['eh'=8,'el'=8,'fsdp'=16] {'fsdp'}, dimensions={0} | all-to-all | bytes 4063232 | tf_op jit(solution)/shard_map/all_to_all | solution.py:399
  94.2 0.7 hidden.1
  94.9 0.0 copy-start.3
  94.9 13.1 %all_to_all.62.r_ref = bf16[16,168,128]{2,1,0:T(8,128)(2,1)S(1)} all-to-all(bf16[16,168,128]{2,1,0:T(8,128)(2,1)S(1)} %get-tuple-element.38), channel_id=1, replica_groups=mesh['eh'=8,'el'=8,'fsdp'=16] {'fsdp'}, dimensions={0} | all-to-all | bytes 1376256 | tf_op jit(solution)/shard_map/all_to_all | solution.py:399
  108.0 0.5 expert_out.1
  108.5 22.2 %all_to_all.63.r_ref = bf16[8,64,128]{2,1,0:T(8,128)(2,1)S(1)} all-to-all(bf16[8,64,128]{2,1,0:T(8,128)(2,1)S(1)} %get-tuple-element.42), channel_id=1, replica_groups=mesh['eh'=8,'el'=8,'fsdp'=16] {'el'}, dimensions={0} | all-to-all | bytes 262144 | tf_op jit(solution)/shard_map/all_to_all | solution.py:399
  130.7 0.4 combine.1
  131.1 26.5 %all_to_all.64.r_ref = bf16[8,32,128]{2,1,0:T(8,128)(2,1)S(1)} all-to-all(bf16[8,32,128]{2,1,0:T(8,128)(2,1)S(1)} %get-tuple-element.43), channel_id=1, replica_groups=mesh['eh'=8,'el'=8,'fsdp'=16] {'eh'}, dimensions={0} | all-to-all | bytes 131072 | tf_op jit(solution)/shard_map/all_to_all | solution.py:399
  157.6 0.0 copy-done.3
  157.6 0.6 resid.1
  158.2 25.7 %all_to_all.65.r_ref = bf16[8,32,128]{2,1,0:T(8,128)(2,1)S(1)} all-to-all(bf16[8,32,128]{2,1,0:T(8,128)(2,1)S(1)} %get-tuple-element.45), channel_id=1, replica_groups=mesh['eh'=8,'el'=8,'fsdp'=16] {'eh'}, dimensions={0} | all-to-all | bytes 131072 | tf_op jit(solution)/shard_map/all_to_all | solution.py:399
  183.9 0.2 redispatch.1
  184.2 12.7 %all_to_all.66.r_ref = bf16[8,64,128]{2,1,0:T(8,128)(2,1)S(1)} all-to-all(bf16[8,64,128]{2,1,0:T(8,128)(2,1)S(1)} %redispatch.1), channel_id=1, replica_groups=mesh['eh'=8,'el'=8,'fsdp'=16] {'el'}, dimensions={0} | all-to-all | bytes 262144 | tf_op jit(solution)/shard_map/all_to_all | solution.py:399
  196.9 1.3 delta_in.1
  198.2 15.5 %all_to_all.67.r_ref = bf16[16,192,128]{2,1,0:T(8,128)(2,1)S(1)} all-to-all(bf16[16,192,128]{2,1,0:T(8,128)(2,1)S(1)} %get-tuple-element.49), channel_id=1, replica_groups=mesh['eh'=8,'el'=8,'fsdp'=16] {'fsdp'}, dimensions={0} | all-to-all | bytes 1572864 | tf_op jit(solution)/shard_map/all_to_all | solution.py:399
  213.7 0.8 delta.1
  214.4 28.1 %all_to_all.68.r_ref = bf16[16,496,128]{2,1,0:T(8,128)(2,1)S(1)} all-to-all(bf16[16,496,128]{2,1,0:T(8,128)(2,1)S(1)} %get-tuple-element.53), channel_id=1, replica_groups=mesh['eh'=8,'el'=8,'fsdp'=16] {'fsdp'}, dimensions={0} | all-to-all | bytes 4063232 | tf_op jit(solution)/shard_map/all_to_all | solution.py:399
  242.5 0.0 copy-start.4
  242.5 1.1 back.1
  243.6 12.5 %all_to_all.69.r_ref = bf16[8,64,128]{2,1,0:T(8,128)(2,1)S(1)} all-to-all(bf16[8,64,128]{2,1,0:T(8,128)(2,1)S(1)} %get-tuple-element.55), channel_id=1, replica_groups=mesh['eh'=8,'el'=8,'fsdp'=16] {'el'}, dimensions={0} | all-to-all | bytes 262144 | tf_op jit(solution)/shard_map/all_to_all | solution.py:399
  256.1 1.1 combine_back.1
  257.2 3.4 %all-to-all-start.11 = ((bf16[8,40,128]{2,1,0:T(8,128)(2,1)}), bf16[8,40,128]{2,1,0:T(8,128)(2,1)S(1)}, u32[]{:S(2)}, u32[]{:S(2)}) async-start(bf16[8,40,128]{2,1,0:T(8,128)(2,1)} %get-tuple-element.56), calls=%async_computation.11 | async-start | bytes 163840 | tf_op jit(solution)/shard_map/all_to_all | solution.py:399
  260.6 1.3 grads.1
  261.9 20.8 %all-to-all-done.11.r_ref = bf16[8,40,128]{2,1,0:T(8,128)(2,1)S(1)} async-done(((bf16[8,40,128]{2,1,0:T(8,128)(2,1)}), bf16[8,40,128]{2,1,0:T(8,128)(2,1)S(1)}, u32[]{:S(2)}, u32[]{:S(2)}) %all-to-all-start.11) | async-done | bytes 81952 | tf_op jit(solution)/shard_map/all_to_all | solution.py:399
  282.7 0.0 copy-done.4
  282.7 0.7 finish.1
  (1 shorter events, 0.0 us)
Async XLA Ops:
  26.0 39.8 %all-to-all-start.1 = ((bf16[8,64,128]{2,1,0:T(8,128)(2,1)}), bf16[8,64,128]{2,1,0:T(8,128)(2,1)S(1)}, u32[]{:S(2)}, u32[]{:S(2)}) async-start(bf16[8,64,128]{2,1,0:T(8,128)(2,1)} %dispatch.1), calls=%async_computation.1 | async-start | bytes 262144 | tf_op jit(solution)/shard_map/all_to_all | solution.py:399
  41.4 0.9 copy-start
  42.3 0.9 copy-start.1
  43.3 0.9 copy-start.2
  94.9 62.7 %copy-start.3 = (bf16[32,128]{1,0:T(8,128)(2,1)S(1)}, bf16[32,128]{1,0:T(8,128)(2,1)}, u32[]{:S(2)}) copy-start(bf16[32,128]{1,0:T(8,128)(2,1)} %t_ref.1) | copy-start | bytes 24580
  242.5 40.2 %copy-start.4 = (s32[32,8]{0,1:T(8,128)S(1)}, s32[32,8]{0,1:T(8,128)}, u32[]{:S(2)}) copy-start(s32[32,8]{0,1:T(8,128)} %param.9) | copy-start | bytes 3076
  257.2 25.5 %all-to-all-start.11 = ((bf16[8,40,128]{2,1,0:T(8,128)(2,1)}), bf16[8,40,128]{2,1,0:T(8,128)(2,1)S(1)}, u32[]{:S(2)}, u32[]{:S(2)}) async-start(bf16[8,40,128]{2,1,0:T(8,128)(2,1)} %get-tuple-element.56), calls=%async_computation.11 | async-start | bytes 163840 | tf_op jit(solution)/shard_map/all_to_all | solution.py:399

commit v6 on v4

--- a/solution.py
+++ b/solution.py
@@ -249,7 +249,7 @@
 def redispatch_body(r_ref, p_ref, m_ref):
     x = jnp.concatenate([r_ref[i] for i in range(r_ref.shape[0])], axis=0)
     for e in range(p_ref.shape[0]):
-        m_ref[e] = dot(p_ref[e], x).astype(BF)
+        m_ref[e] = dot(p_ref[e], x)[: m_ref.shape[1]].astype(BF)
 
 
 def delta_in_body(r_ref, w_ref, out_ref, wd_ref, h_ref, f_ref, g_ref):
@@ -270,12 +270,14 @@
         jnp.concatenate(tiles[half:], axis=0), 88
     )
     packed = jnp.concatenate([packed, jnp.zeros((fs - packed.shape[0], LANES), F4)], axis=0)
+    parts = dot(wd_ref[...], scaled, 1, 1)
+    down = dot(h_ref[...], scaled)
     for d in range(n):
-        part = dot(wd_ref[d * fs : (d + 1) * fs], scaled, 1, 1)
+        part = parts[d * fs : (d + 1) * fs]
         message = blocks_to_rows(part)
         last = message[3 * fs :] + packed
         f_ref[d] = jnp.concatenate([message[: 3 * fs], last], axis=0).astype(BF)
-        g_ref[d] = dot(h_ref[d * fs : (d + 1) * fs], scaled).astype(BF)
+        g_ref[d] = down[d * fs : (d + 1) * fs].astype(BF)
 
 
 def delta_body(r_ref, gate_ref, up_ref, wgu_ref, gd_ref, f_ref, dgu_ref, dot_ref):
@@ -432,7 +434,7 @@
     )
     got = exchange(message, "eh")
     (message,) = call(
-        redispatch_body, [((l, 8 * h, df), BF)], got, place, name="redispatch"
+        redispatch_body, [((l, CAP * h, df), BF)], got, place, name="redispatch"
     )
     got = exchange(message, "el")
     message, down = call(

time: 284 us -> 283 us (level)
  no operation moved by 1% of the time
where the time goes in v6:
time: 283 us; the launch traced here: 279 us
  blocking collectives  229 us (81%)
  waiting for transfers between devices  23.8 us (8%)
  starting transfers between devices  11.9 us (4%)
  Pallas kernels  10.9 us (4%)
    all_to_all x10, blocking collectives, exchange(): return lax.all_to_all(x, axis, split_axis=0, concat_axis=0, tiled=True)  229 us
    all_to_all x2, waiting for transfers between devices, exchange(): return lax.all_to_all(x, axis, split_axis=0, concat_axis=0, tiled=True)  23.8 us
    all_to_all x2, starting transfers between devices, exchange(): return lax.all_to_all(x, axis, split_axis=0, concat_axis=0, tiled=True)  11.9 us
    pallas_call x15, Pallas kernels, call(): pl.pallas_call(body, out_shape=shapes, in_specs=specs, out_specs=[pl.Bloc...  10.9 us
  transfers between devices with their start and end apart: 2, of which 2 were waited for; matrix products, arithmetic and copies ran while one was open for 0% of the time, Pallas kernels for 0%

profile of v6, /device:TPU:1, one launch (start us, length us, event | category | flops | bytes accessed | tf_op | source)
XLA Modules:
  0.0 279.2 jit_solution(9496360669688948238)
XLA Ops:
  0.6 1.5 first.1
  2.2 51.2 %all_to_all.60.r_ref = bf16[8,40,128]{2,1,0:T(8,128)(2,1)S(1)} all-to-all(bf16[8,40,128]{2,1,0:T(8,128)(2,1)} %first.1), channel_id=1, replica_groups=mesh['eh'=8,'el'=8,'fsdp'=16] {'eh'}, dimensions={0} | all-to-all | bytes 163840 | tf_op jit(solution)/shard_map/all_to_all | solution.py:376
  53.4 1.1 dispatch.1
  54.5 8.5 %all-to-all-start.1 = ((bf16[8,64,128]{2,1,0:T(8,128)(2,1)}), bf16[8,64,128]{2,1,0:T(8,128)(2,1)S(1)}, u32[]{:S(2)}, u32[]{:S(2)}) async-start(bf16[8,64,128]{2,1,0:T(8,128)(2,1)} %get-tuple-element.35), calls=%async_computation.1 | async-start | bytes 262144 | tf_op jit(solution)/shard_map/all_to_all | solution.py:376
  63.0 0.0 copy-start
  63.0 0.9 copy-done
  63.9 0.0 copy-start.1
  63.9 0.9 copy-done.1
  64.8 0.0 copy-start.2
  64.8 0.9 copy-done.2
  65.8 3.0 %all-to-all-done.1.r_ref = bf16[8,64,128]{2,1,0:T(8,128)(2,1)S(1)} async-done(((bf16[8,64,128]{2,1,0:T(8,128)(2,1)}), bf16[8,64,128]{2,1,0:T(8,128)(2,1)S(1)}, u32[]{:S(2)}, u32[]{:S(2)}) %all-to-all-start.1) | async-done | bytes 131104 | tf_op jit(solution)/shard_map/all_to_all | solution.py:376
  68.8 0.3 expert_in.1
  69.1 32.1 %all_to_all.61.r_ref.x_ref = bf16[16,496,128]{2,1,0:T(8,128)(2,1)S(1)} all-to-all(bf16[16,496,128]{2,1,0:T(8,128)(2,1)S(1)} %get-tuple-element.37), channel_id=1, replica_groups=mesh['eh'=8,'el'=8,'fsdp'=16] {'fsdp'}, dimensions={0} | all-to-all | bytes 4063232 | tf_op jit(solution)/shard_map/all_to_all | solution.py:376
  101.2 0.7 hidden.1
  101.9 0.0 copy-start.3
  101.9 14.9 %all_to_all.62.r_ref = bf16[16,168,128]{2,1,0:T(8,128)(2,1)S(1)} all-to-all(bf16[16,168,128]{2,1,0:T(8,128)(2,1)S(1)} %get-tuple-element.39), channel_id=1, replica_groups=mesh['eh'=8,'el'=8,'fsdp'=16] {'fsdp'}, dimensions={0} | all-to-all | bytes 1376256 | tf_op jit(solution)/shard_map/all_to_all | solution.py:376
  116.8 0.5 expert_out.1
  117.3 11.7 %all_to_all.63.r_ref = bf16[8,64,128]{2,1,0:T(8,128)(2,1)S(1)} all-to-all(bf16[8,64,128]{2,1,0:T(8,128)(2,1)S(1)} %get-tuple-element.42), channel_id=1, replica_groups=mesh['eh'=8,'el'=8,'fsdp'=16] {'el'}, dimensions={0} | all-to-all | bytes 262144 | tf_op jit(solution)/shard_map/all_to_all | solution.py:376
  129.0 0.3 combine.1
  129.2 24.4 %all_to_all.64.r_ref = bf16[8,32,128]{2,1,0:T(8,128)(2,1)S(1)} all-to-all(bf16[8,32,128]{2,1,0:T(8,128)(2,1)S(1)} %combine.1), channel_id=1, replica_groups=mesh['eh'=8,'el'=8,'fsdp'=16] {'eh'}, dimensions={0} | all-to-all | bytes 131072 | tf_op jit(solution)/shard_map/all_to_all | solution.py:376
  153.7 0.0 copy-done.3
  153.7 0.6 resid.1
  154.3 25.8 %all_to_all.65.r_ref = bf16[8,32,128]{2,1,0:T(8,128)(2,1)S(1)} all-to-all(bf16[8,32,128]{2,1,0:T(8,128)(2,1)S(1)} %get-tuple-element.45), channel_id=1, replica_groups=mesh['eh'=8,'el'=8,'fsdp'=16] {'eh'}, dimensions={0} | all-to-all | bytes 131072 | tf_op jit(solution)/shard_map/all_to_all | solution.py:376
  180.1 0.2 redispatch.1
  180.3 13.2 %all_to_all.66.r_ref = bf16[8,56,128]{2,1,0:T(8,128)(2,1)S(1)} all-to-all(bf16[8,56,128]{2,1,0:T(8,128)(2,1)S(1)} %redispatch.1), channel_id=1, replica_groups=mesh['eh'=8,'el'=8,'fsdp'=16] {'el'}, dimensions={0} | all-to-all | bytes 229376 | tf_op jit(solution)/shard_map/all_to_all | solution.py:376
  193.5 0.7 delta_in.1
  194.2 15.7 %all_to_all.67.r_ref = bf16[16,192,128]{2,1,0:T(8,128)(2,1)S(1)} all-to-all(bf16[16,192,128]{2,1,0:T(8,128)(2,1)S(1)} %get-tuple-element.48), channel_id=1, replica_groups=mesh['eh'=8,'el'=8,'fsdp'=16] {'fsdp'}, dimensions={0} | all-to-all | bytes 1572864 | tf_op jit(solution)/shard_map/all_to_all | solution.py:376
  209.8 0.8 delta.1
  210.6 28.1 %all_to_all.68.r_ref = bf16[16,496,128]{2,1,0:T(8,128)(2,1)S(1)} all-to-all(bf16[16,496,128]{2,1,0:T(8,128)(2,1)S(1)} %get-tuple-element.52), channel_id=1, replica_groups=mesh['eh'=8,'el'=8,'fsdp'=16] {'fsdp'}, dimensions={0} | all-to-all | bytes 4063232 | tf_op jit(solution)/shard_map/all_to_all | solution.py:376
  238.7 1.1 back.1
  239.9 12.1 %all_to_all.69.r_ref = bf16[8,64,128]{2,1,0:T(8,128)(2,1)S(1)} all-to-all(bf16[8,64,128]{2,1,0:T(8,128)(2,1)S(1)} %get-tuple-element.54), channel_id=1, replica_groups=mesh['eh'=8,'el'=8,'fsdp'=16] {'el'}, dimensions={0} | all-to-all | bytes 262144 | tf_op jit(solution)/shard_map/all_to_all | solution.py:376
  252.0 1.1 combine_back.1
  253.1 3.4 %all-to-all-start.11 = ((bf16[8,40,128]{2,1,0:T(8,128)(2,1)}), bf16[8,40,128]{2,1,0:T(8,128)(2,1)S(1)}, u32[]{:S(2)}, u32[]{:S(2)}) async-start(bf16[8,40,128]{2,1,0:T(8,128)(2,1)} %get-tuple-element.56), calls=%async_computation.11 | async-start | bytes 163840 | tf_op jit(solution)/shard_map/all_to_all | solution.py:376
  256.5 1.3 grads.1
  257.7 20.8 %all-to-all-done.11.r_ref = bf16[8,40,128]{2,1,0:T(8,128)(2,1)S(1)} async-done(((bf16[8,40,128]{2,1,0:T(8,128)(2,1)}), bf16[8,40,128]{2,1,0:T(8,128)(2,1)S(1)}, u32[]{:S(2)}, u32[]{:S(2)}) %all-to-all-start.11) | async-done | bytes 81952 | tf_op jit(solution)/shard_map/all_to_all | solution.py:376
  278.6 0.7 finish.1
  (1 shorter events, 0.0 us)
Async XLA Ops:
  54.5 14.3 %all-to-all-start.1 = ((bf16[8,64,128]{2,1,0:T(8,128)(2,1)}), bf16[8,64,128]{2,1,0:T(8,128)(2,1)S(1)}, u32[]{:S(2)}, u32[]{:S(2)}) async-start(bf16[8,64,128]{2,1,0:T(8,128)(2,1)} %get-tuple-element.35), calls=%async_computation.1 | async-start | bytes 262144 | tf_op jit(solution)/shard_map/all_to_all | solution.py:376
  63.0 0.9 copy-start
  63.9 0.9 copy-start.1
  64.8 0.9 copy-start.2
  101.9 51.8 %copy-start.3 = (bf16[32,128]{1,0:T(8,128)(2,1)S(1)}, bf16[32,128]{1,0:T(8,128)(2,1)}, u32[]{:S(2)}) copy-start(bf16[32,128]{1,0:T(8,128)(2,1)} %t_ref.1) | copy-start | bytes 24580
  253.1 25.5 %all-to-all-start.11 = ((bf16[8,40,128]{2,1,0:T(8,128)(2,1)}), bf16[8,40,128]{2,1,0:T(8,128)(2,1)S(1)}, u32[]{:S(2)}, u32[]{:S(2)}) async-start(bf16[8,40,128]{2,1,0:T(8,128)(2,1)} %get-tuple-element.56), calls=%async_computation.11 | async-start | bytes 163840 | tf_op jit(solution)/shard_map/all_to_all | solution.py:376

commit v7 on v6

--- a/solution.py
+++ b/solution.py
@@ -111,14 +111,15 @@
         m_ref[i] = message
 
 
-def weights_body(wg_ref, wu_ref, wd_ref, wgu_ref, wd_out_ref):
+def weights_body(wg_ref, wu_ref, wd_ref, wgu_ref, wd_out_ref, tick_ref):
     fs = wg_ref.shape[0]
     wgu_ref[:fs] = wg_ref[...]
     wgu_ref[fs:] = wu_ref[...]
     wd_out_ref[...] = wd_ref[...]
-
-
-def dispatch_body(base_ref, r_ref, m_ref, p_ref, ids_ref):
+    tick_ref[...] = jnp.zeros_like(tick_ref)
+
+
+def dispatch_body(base_ref, r_ref, tick_ref, m_ref, p_ref, ids_ref):
     h, l = r_ref.shape[0], m_ref.shape[0]
     g = 32
     width = h * g
@@ -398,13 +399,13 @@
         vmem_mib=60, name="first",
     )
     got = exchange(message, "eh")
-    wgu, wd = call(
-        weights_body, [((2 * fs, d), BF), ((fs, d), BF)], wg, wu, wd, name="weights"
+    wgu, wd, tick = call(
+        weights_body, [((2 * fs, d), BF), ((fs, d), BF), ((8, LANES), F4)], wg, wu, wd, name="weights"
     )
     message, place, ids = call(
         dispatch_body,
         [((l, 8 * h, df), BF), ((l, 8 * h, h * g), BF), ((8, h * g), F4)],
-        base, got, smem=(0,), name="dispatch",
+        base, got, tick, smem=(0,), name="dispatch",
     )
     got = exchange(message, "el")
     message, w_tile = call(

time: 283 us -> 282 us (level)
  blocking collectives: 229 us -> 192 us
  starting transfers between devices: 11.9 us -> 32.3 us
  waiting for transfers between devices: 23.8 us -> 40.3 us
    all_to_all x10, blocking collectives: 229 us -> 192 us  [exchange(): return lax.all_to_all(x, axis, split_axis=0, concat_axis=0, tiled=True)]
    all_to_all x2, starting transfers between devices: 11.9 us -> 32.3 us  [exchange(): return lax.all_to_all(x, axis, split_axis=0, concat_axis=0, tiled=True)]
    all_to_all x2, waiting for transfers between devices: 23.8 us -> 40.3 us  [exchange(): return lax.all_to_all(x, axis, split_axis=0, concat_axis=0, tiled=True)]
where the time goes in v7:
time: 282 us; the launch traced here: 278 us
  blocking collectives  192 us (68%)
  waiting for transfers between devices  40.3 us (14%)
  starting transfers between devices  32.3 us (11%)
  Pallas kernels  10.3 us (4%)
    all_to_all x10, blocking collectives, exchange(): return lax.all_to_all(x, axis, split_axis=0, concat_axis=0, tiled=True)  192 us
    all_to_all x2, waiting for transfers between devices, exchange(): return lax.all_to_all(x, axis, split_axis=0, concat_axis=0, tiled=True)  40.3 us
    all_to_all x2, starting transfers between devices, exchange(): return lax.all_to_all(x, axis, split_axis=0, concat_axis=0, tiled=True)  32.3 us
    pallas_call x15, Pallas kernels, call(): pl.pallas_call(body, out_shape=shapes, in_specs=specs, out_specs=[pl.Bloc...  10.3 us
  transfers between devices with their start and end apart: 2, of which 2 were waited for; matrix products, arithmetic and copies ran while one was open for 0% of the time, Pallas kernels for 0%

profile of v7, /device:TPU:1, one launch (start us, length us, event | category | flops | bytes accessed | tf_op | source)
XLA Modules:
  0.0 278.3 jit_solution(7197762054947829266)
XLA Ops:
  0.6 1.5 first.1
  2.2 28.9 %all-to-all-start = ((bf16[8,40,128]{2,1,0:T(8,128)(2,1)}), bf16[8,40,128]{2,1,0:T(8,128)(2,1)S(1)}, u32[]{:S(2)}, u32[]{:S(2)}) async-start(bf16[8,40,128]{2,1,0:T(8,128)(2,1)} %first.1), calls=%async_computation | async-start | bytes 163840 | tf_op jit(solution)/shard_map/all_to_all | solution.py:377
  31.1 0.0 copy-start
  31.1 0.9 copy-done
  32.0 0.0 copy-start.1
  32.0 0.9 copy-done.1
  32.9 0.0 copy-start.2
  32.9 0.9 copy-done.2
  33.9 19.5 %all-to-all-done.r_ref = bf16[8,40,128]{2,1,0:T(8,128)(2,1)S(1)} async-done(((bf16[8,40,128]{2,1,0:T(8,128)(2,1)}), bf16[8,40,128]{2,1,0:T(8,128)(2,1)S(1)}, u32[]{:S(2)}, u32[]{:S(2)}) %all-to-all-start) | async-done | bytes 81952 | tf_op jit(solution)/shard_map/all_to_all | solution.py:377
  53.4 0.5 dispatch.1
  53.8 14.1 %all_to_all.60.r_ref = bf16[8,64,128]{2,1,0:T(8,128)(2,1)S(1)} all-to-all(bf16[8,64,128]{2,1,0:T(8,128)(2,1)S(1)} %get-tuple-element.37), channel_id=1, replica_groups=mesh['eh'=8,'el'=8,'fsdp'=16] {'el'}, dimensions={0} | all-to-all | bytes 262144 | tf_op jit(solution)/shard_map/all_to_all | solution.py:377
  67.9 0.3 expert_in.1
  68.2 32.1 %all_to_all.61.r_ref.x_ref = bf16[16,496,128]{2,1,0:T(8,128)(2,1)S(1)} all-to-all(bf16[16,496,128]{2,1,0:T(8,128)(2,1)S(1)} %get-tuple-element.39), channel_id=1, replica_groups=mesh['eh'=8,'el'=8,'fsdp'=16] {'fsdp'}, dimensions={0} | all-to-all | bytes 4063232 | tf_op jit(solution)/shard_map/all_to_all | solution.py:377
  100.3 0.7 hidden.1
  101.0 0.0 copy-start.3
  101.1 14.9 %all_to_all.62.r_ref = bf16[16,168,128]{2,1,0:T(8,128)(2,1)S(1)} all-to-all(bf16[16,168,128]{2,1,0:T(8,128)(2,1)S(1)} %get-tuple-element.41), channel_id=1, replica_groups=mesh['eh'=8,'el'=8,'fsdp'=16] {'fsdp'}, dimensions={0} | all-to-all | bytes 1376256 | tf_op jit(solution)/shard_map/all_to_all | solution.py:377
  115.9 0.5 expert_out.1
  116.4 11.7 %all_to_all.63.r_ref = bf16[8,64,128]{2,1,0:T(8,128)(2,1)S(1)} all-to-all(bf16[8,64,128]{2,1,0:T(8,128)(2,1)S(1)} %get-tuple-element.44), channel_id=1, replica_groups=mesh['eh'=8,'el'=8,'fsdp'=16] {'el'}, dimensions={0} | all-to-all | bytes 262144 | tf_op jit(solution)/shard_map/all_to_all | solution.py:377
  128.1 0.3 combine.1
  128.4 24.4 %all_to_all.64.r_ref = bf16[8,32,128]{2,1,0:T(8,128)(2,1)S(1)} all-to-all(bf16[8,32,128]{2,1,0:T(8,128)(2,1)S(1)} %combine.1), channel_id=1, replica_groups=mesh['eh'=8,'el'=8,'fsdp'=16] {'eh'}, dimensions={0} | all-to-all | bytes 131072 | tf_op jit(solution)/shard_map/all_to_all | solution.py:377
  152.8 0.0 copy-done.3
  152.8 0.6 resid.1
  153.4 25.9 %all_to_all.65.r_ref = bf16[8,32,128]{2,1,0:T(8,128)(2,1)S(1)} all-to-all(bf16[8,32,128]{2,1,0:T(8,128)(2,1)S(1)} %get-tuple-element.47), channel_id=1, replica_groups=mesh['eh'=8,'el'=8,'fsdp'=16] {'eh'}, dimensions={0} | all-to-all | bytes 131072 | tf_op jit(solution)/shard_map/all_to_all | solution.py:377
  179.3 0.2 redispatch.1
  179.5 13.1 %all_to_all.66.r_ref = bf16[8,56,128]{2,1,0:T(8,128)(2,1)S(1)} all-to-all(bf16[8,56,128]{2,1,0:T(8,128)(2,1)S(1)} %redispatch.1), channel_id=1, replica_groups=mesh['eh'=8,'el'=8,'fsdp'=16] {'el'}, dimensions={0} | all-to-all | bytes 229376 | tf_op jit(solution)/shard_map/all_to_all | solution.py:377
  192.6 0.7 delta_in.1
  193.3 15.6 %all_to_all.67.r_ref = bf16[16,192,128]{2,1,0:T(8,128)(2,1)S(1)} all-to-all(bf16[16,192,128]{2,1,0:T(8,128)(2,1)S(1)} %get-tuple-element.50), channel_id=1, replica_groups=mesh['eh'=8,'el'=8,'fsdp'=16] {'fsdp'}, dimensions={0} | all-to-all | bytes 1572864 | tf_op jit(solution)/shard_map/all_to_all | solution.py:377
  208.9 0.8 delta.1
  209.7 28.1 %all_to_all.68.r_ref = bf16[16,496,128]{2,1,0:T(8,128)(2,1)S(1)} all-to-all(bf16[16,496,128]{2,1,0:T(8,128)(2,1)S(1)} %get-tuple-element.54), channel_id=1, replica_groups=mesh['eh'=8,'el'=8,'fsdp'=16] {'fsdp'}, dimensions={0} | all-to-all | bytes 4063232 | tf_op jit(solution)/shard_map/all_to_all | solution.py:377
  237.8 1.1 back.1
  238.9 12.1 %all_to_all.69.r_ref = bf16[8,64,128]{2,1,0:T(8,128)(2,1)S(1)} all-to-all(bf16[8,64,128]{2,1,0:T(8,128)(2,1)S(1)} %get-tuple-element.56), channel_id=1, replica_groups=mesh['eh'=8,'el'=8,'fsdp'=16] {'el'}, dimensions={0} | all-to-all | bytes 262144 | tf_op jit(solution)/shard_map/all_to_all | solution.py:377
  251.0 1.1 combine_back.1
  252.2 3.4 %all-to-all-start.11 = ((bf16[8,40,128]{2,1,0:T(8,128)(2,1)}), bf16[8,40,128]{2,1,0:T(8,128)(2,1)S(1)}, u32[]{:S(2)}, u32[]{:S(2)}) async-start(bf16[8,40,128]{2,1,0:T(8,128)(2,1)} %get-tuple-element.58), calls=%async_computation.11 | async-start | bytes 163840 | tf_op jit(solution)/shard_map/all_to_all | solution.py:377
  255.5 1.3 grads.1
  256.8 20.8 %all-to-all-done.11.r_ref = bf16[8,40,128]{2,1,0:T(8,128)(2,1)S(1)} async-done(((bf16[8,40,128]{2,1,0:T(8,128)(2,1)}), bf16[8,40,128]{2,1,0:T(8,128)(2,1)S(1)}, u32[]{:S(2)}, u32[]{:S(2)}) %all-to-all-start.11) | async-done | bytes 81952 | tf_op jit(solution)/shard_map/all_to_all | solution.py:377
  277.6 0.7 finish.1
  (1 shorter events, 0.0 us)
Async XLA Ops:
  2.2 51.2 %all-to-all-start = ((bf16[8,40,128]{2,1,0:T(8,128)(2,1)}), bf16[8,40,128]{2,1,0:T(8,128)(2,1)S(1)}, u32[]{:S(2)}, u32[]{:S(2)}) async-start(bf16[8,40,128]{2,1,0:T(8,128)(2,1)} %first.1), calls=%async_computation | async-start | bytes 163840 | tf_op jit(solution)/shard_map/all_to_all | solution.py:377
  31.1 0.9 copy-start
  32.0 0.9 copy-start.1
  32.9 0.9 copy-start.2
  101.0 51.7 %copy-start.3 = (bf16[32,128]{1,0:T(8,128)(2,1)S(1)}, bf16[32,128]{1,0:T(8,128)(2,1)}, u32[]{:S(2)}) copy-start(bf16[32,128]{1,0:T(8,128)(2,1)} %t_ref.1) | copy-start | bytes 24580
  252.2 25.5 %all-to-all-start.11 = ((bf16[8,40,128]{2,1,0:T(8,128)(2,1)}), bf16[8,40,128]{2,1,0:T(8,128)(2,1)S(1)}, u32[]{:S(2)}, u32[]{:S(2)}) async-start(bf16[8,40,128]{2,1,0:T(8,128)(2,1)} %get-tuple-element.58), calls=%async_computation.11 | async-start | bytes 163840 | tf_op jit(solution)/shard_map/all_to_all | solution.py:377
